TPU v7x, 32 devices: a whole 2x2x4 slice. The times are simulated.
32 devices in a mesh: circ: 8 (over z, x), ax: 4 (over y, core).
Axes of the slice: x: 2, y: 2, z: 4, core: 2. Of those that a mesh axis runs over, the one named last changes fastest.
Arguments:
- fields: float32 [3, 8, 64, 1024], P(None, None, 'circ', 'ax'), may hold values from -6 to 6
Outputs:
- deriv_circ: float32 [3, 8, 64, 1024], P(None, None, 'circ', 'ax')
- deriv_axial: float32 [3, 8, 64, 1024], P(None, None, 'circ', 'ax')
- filtered: float32 [3, 8, 64, 1024], P(None, None, 'circ', 'ax')
All inputs are finite; a program needn't handle non-finite values.
Results may differ from a plain program's by a relative error of at most 0.0003.
Values sent between devices are 32-bit elements; how exact they have to be, the bound alone decides.
A program may use at most 64 MiB of HBM per device.

v0:
```python
import math

import jax
import jax.numpy as jnp
import numpy as np
from jax import lax
from jax.sharding import PartitionSpec as P

DERIV_NEAR = 14.0 / 9.0
DERIV_FAR = 1.0 / 9.0
ALPHA_DERIV = 1.0 / 3.0
ALPHA_FILTER = 0.4999
PRECISE = lax.Precision.HIGHEST


def with_halo(value, sides, width, wrap):
    for axis, dim in sides:
        peers, length = (lax.axis_size(axis), value.shape[dim])
        up = [(i, (i + 1) % peers) for i in range(peers if wrap else peers - 1)]
        down = [(j, i) for i, j in up]
        last = lax.slice_in_dim(value, length - width, length, axis=dim)
        initial = lax.slice_in_dim(value, 0, width, axis=dim)
        before = lax.ppermute(last, axis, up)
        after = lax.ppermute(initial, axis, down)
        value = jnp.concatenate([before, value, after], axis=dim)
    return value


def entering_2(part, axis, combine, identity, reverse):
    count = lax.axis_size(axis)
    place = lax.axis_index(axis)
    ahead = count - 1 - place if reverse else place
    gathered = jax.tree.map(lambda a: lax.all_gather(a, axis), part)
    state = jax.tree.map(lambda a, e: jnp.zeros_like(a) + jnp.asarray(e, a.dtype), part, identity)

    def one(step, state):
        source = count - 1 - step if reverse else step
        return combine(
            state, jax.tree.map(lambda a: lax.dynamic_index_in_dim(a, source, 0, False), gathered)
        )

    return lax.fori_loop(0, ahead, one, state)


def filter_terms(coupling):
    return [
        (193.0 + 126.0 * coupling) / 256.0,
        (105.0 + 302.0 * coupling) / 256.0,
        15.0 * (2.0 * coupling - 1.0) / 64.0,
        45.0 * (1.0 - 2.0 * coupling) / 512.0,
        5.0 * (2.0 * coupling - 1.0) / 256.0,
        (1.0 - 2.0 * coupling) / 512.0,
    ]


def root_of(coupling):
    return (-1.0 + math.sqrt(1.0 - 4.0 * coupling * coupling)) / (2.0 * coupling)


def signed_power(exponent, log_sizes):
    magnitude = jnp.exp(exponent[..., None].astype(jnp.float32) * log_sizes)
    parity = (exponent % 2).astype(jnp.float32)
    return magnitude * (1.0 - 2.0 * parity)[..., None]


def affine_chain(earlier, later):
    return (earlier[0] * later[0], later[0] * earlier[1] + later[1])


def running_products(values):
    result = np.zeros(len(values))
    running = 1.0
    for place in range(len(values)):
        running = running * values[place]
        result[place] = running
    return result


def axial_rhs(shifted, row_index, line_length):
    interior = 0.5 * DERIV_NEAR * (shifted(1) - shifted(-1)) + 0.25 * DERIV_FAR * (
        shifted(2) - shifted(-2)
    )
    row_opening = -2.5 * shifted(0) + 2.0 * shifted(1) + 0.5 * shifted(2)
    row_second = 0.75 * (shifted(1) - shifted(-1))
    row_closing = 2.5 * shifted(0) - 2.0 * shifted(-1) - 0.5 * shifted(-2)
    result = jnp.where(row_index == 0, row_opening, interior)
    result = jnp.where((row_index == 1) | (row_index == line_length - 2), row_second, result)
    return jnp.where(row_index == line_length - 1, row_closing, result)


def bands_table(line_length):
    band_lower = np.full(line_length, ALPHA_DERIV)
    band_lower[0] = 0.0
    band_lower[1] = 0.25
    band_lower[line_length - 2] = 0.25
    band_lower[line_length - 1] = 2.0
    band_middle = np.ones(line_length)
    band_upper = np.full(line_length, ALPHA_DERIV)
    band_upper[0] = 2.0
    band_upper[1] = 0.25
    band_upper[line_length - 2] = 0.25
    band_upper[line_length - 1] = 0.0
    return (band_lower, band_middle, band_upper)


def thomas_tables(line_cells, axial_count):
    line_length = line_cells * axial_count
    band_lower, band_middle, band_upper = bands_table(line_length)
    pivots = np.zeros(line_length)
    factors = np.zeros(line_length)
    pivots[0] = band_middle[0]
    for row_number in range(1, line_length):
        factors[row_number] = -band_lower[row_number] / pivots[row_number - 1]
        pivots[row_number] = (
            band_middle[row_number] + factors[row_number] * band_upper[row_number - 1]
        )
    backs = -band_upper / pivots
    fwd_blocks, fwd_grows, back_blocks, back_grows, inv_pivots = ([], [], [], [], [])
    for place in range(axial_count):
        base_row = place * line_cells
        seg_fwd = factors[base_row : base_row + line_cells]
        seg_back = backs[base_row : base_row + line_cells]
        block_fwd = np.zeros((line_cells, line_cells))
        block_back = np.zeros((line_cells, line_cells))
        for target in range(line_cells):
            running = 1.0
            block_fwd[target, target] = 1.0
            for source in range(target - 1, -1, -1):
                running = running * seg_fwd[source + 1]
                block_fwd[target, source] = running
            running = 1.0
            block_back[target, target] = 1.0
            for source in range(target + 1, line_cells):
                running = running * seg_back[source - 1]
                block_back[target, source] = running
        fwd_blocks.append(block_fwd)
        fwd_grows.append(running_products(seg_fwd))
        back_blocks.append(block_back)
        back_grows.append(running_products(seg_back[::-1])[::-1])
        inv_pivots.append(1.0 / pivots[base_row : base_row + line_cells])
    return [
        jnp.asarray(np.stack(table), jnp.float32)
        for table in (fwd_blocks, fwd_grows, back_blocks, back_grows, inv_pivots)
    ]


def shards(fields):
    cells = fields.shape[2]
    line_cells = fields.shape[3]
    roots = [root_of(ALPHA_DERIV), root_of(ALPHA_FILTER)]
    circ_count = lax.axis_size("circ")
    circ_place = lax.axis_index("circ")
    loop_cells = cells * circ_count
    log_sizes = jnp.asarray([math.log(abs(root_value)) for root_value in roots], jnp.float32)
    wrap_scale = jnp.asarray(
        [1.0 / (1.0 - root_value**loop_cells) for root_value in roots], jnp.float32
    )
    padded = with_halo(fields, (("circ", 2),), 5, True)

    def circ_take(offset):
        return padded[:, :, 5 + offset : 5 + offset + cells, :]

    circ_right = 0.5 * DERIV_NEAR * (circ_take(1) - circ_take(-1)) + 0.25 * DERIV_FAR * (
        circ_take(2) - circ_take(-2)
    )
    terms = filter_terms(ALPHA_FILTER)
    filter_right = terms[0] * circ_take(0)
    for offset in range(1, 6):
        filter_right = filter_right + 0.5 * terms[offset] * (circ_take(offset) + circ_take(-offset))
    scaled = jnp.stack([circ_right * (1.0 + roots[0] ** 2), filter_right * (1.0 + roots[1] ** 2)])
    cell_steps = np.arange(cells)
    cell_gap = cell_steps[:, None] - cell_steps[None, :]
    forward_np = np.stack(
        [
            np.where(cell_gap >= 0, root_value ** np.maximum(cell_gap, 0), 0.0)
            for root_value in roots
        ]
    )
    backward_np = np.stack(
        [
            np.where(cell_gap <= 0, root_value ** np.maximum(-cell_gap, 0), 0.0)
            for root_value in roots
        ]
    )
    forward_table = jnp.asarray(forward_np, jnp.float32)
    backward_table = jnp.asarray(backward_np, jnp.float32)
    grow_forward = jnp.asarray(
        np.stack([root_value ** (cell_steps + 1) for root_value in roots]), jnp.float32
    )
    grow_backward = jnp.asarray(
        np.stack([root_value ** (cells - cell_steps) for root_value in roots]), jnp.float32
    )

    def circ_carry(state, backward):
        piece = lax.all_gather(state[None], "circ", axis=0, tiled=True)
        shard_ids = jnp.arange(piece.shape[0], dtype=jnp.int32)
        if backward:
            distance = (shard_ids - circ_place - 1) % circ_count
        else:
            distance = (circ_place - shard_ids - 1) % circ_count
        weights = signed_power(distance * cells, log_sizes) * wrap_scale
        return jnp.zeros_like(state) + jnp.einsum(
            "qs,qsfna->sfna", weights, piece, precision=PRECISE
        )

    partial_forward = jnp.einsum("sjk,sfnka->sfnja", forward_table, scaled, precision=PRECISE)
    incoming = circ_carry(partial_forward[:, :, :, -1, :], False)
    forward_full = (
        partial_forward + grow_forward[:, None, None, :, None] * incoming[:, :, :, None, :]
    )
    partial_back = jnp.einsum("sjk,sfnka->sfnja", backward_table, forward_full, precision=PRECISE)
    incoming_back = circ_carry(partial_back[:, :, :, 0, :], True)
    solved = partial_back + grow_backward[:, None, None, :, None] * incoming_back[:, :, :, None, :]
    deriv_circ = solved[0]
    filtered = solved[1]
    axial_count = lax.axis_size("ax")
    axial_place = lax.axis_index("ax")
    line_length = line_cells * axial_count
    padded_axial = with_halo(fields, (("ax", 3),), 2, False)

    def axial_take(offset):
        return padded_axial[:, :, :, 2 + offset : 2 + offset + line_cells]

    global_rows = axial_place * line_cells + jnp.arange(line_cells, dtype=jnp.int32)
    axial_right = axial_rhs(axial_take, global_rows, line_length)
    tables = thomas_tables(line_cells, axial_count)
    fwd_block, fwd_grow, back_block, back_grow, inv_pivot = [
        lax.dynamic_index_in_dim(table, axial_place, 0, keepdims=False) for table in tables
    ]

    def axial_carry(multiplier, state, backward):
        identity = (jnp.ones_like(multiplier), jnp.zeros_like(state))
        return entering_2((multiplier, state), "ax", affine_chain, identity, backward)[1]

    local_fwd = jnp.einsum("fnck,jk->fncj", axial_right, fwd_block, precision=PRECISE)
    entering = axial_carry(fwd_grow[-1].reshape(1, 1, 1), local_fwd[:, :, :, -1], False)
    eliminated = (local_fwd + fwd_grow * entering[:, :, :, None]) * inv_pivot
    local_back = jnp.einsum("fnck,jk->fncj", eliminated, back_block, precision=PRECISE)
    entering_back = axial_carry(back_grow[0].reshape(1, 1, 1), local_back[:, :, :, 0], True)
    deriv_axial = local_back + back_grow * entering_back[:, :, :, None]
    return (deriv_circ, deriv_axial, filtered)


def solution(mesh):
    placed = (P(None, None, "circ", "ax"),)
    return jax.shard_map(
        shards,
        mesh=mesh,
        in_specs=placed,
        out_specs=(
            P(None, None, "circ", "ax"),
            P(None, None, "circ", "ax"),
            P(None, None, "circ", "ax"),
        ),
        check_vma=False,
    )
```

profile of v0, /device:TPU:0, one launch (start us, length us, event | category | flops | bytes accessed | tf_op | source)
XLA Modules:
  0.0 115.6 jit_solution(11230876055977664104)
XLA Ops:
  0.6 1.1 fusion.99
  1.7 6.0 %collective-permute-start = (f32[3,8,5,256]{3,2,1,0:T(8,128)S(1)}, f32[3,8,5,256]{3,2,1,0:T(8,128)S(1)}, u32[]{:S(2)}, u32[]{:S(2)}) collective-permute-start(f32[3,8,5,256]{3,2,1,0:T(8,128)S(1)} %get-tuple-element.162), channel_id=1, source_target_pairs={{4,0},{8,4},{12,8},{16,12},{20,16},{24,20},{28,24},{0,28},{5,1},{9... | collective-permute-start | bytes 368648 | tf_op jit(solution)/shard_map/ppermute | solution.py:24
  7.8 0.1 fusion.98
  7.9 1.3 %collective-permute-start.3 = (f32[3,8,8,2]{3,2,1,0:T(8,128)S(1)}, f32[3,8,8,2]{3,2,1,0:T(8,128)S(1)}, u32[]{:S(2)}, u32[]{:S(2)}) collective-permute-start(f32[3,8,8,2]{3,2,1,0:T(8,128)S(1)} %get-tuple-element.160), channel_id=1, source_target_pairs={{1,0},{2,1},{3,2},{5,4},{6,5},{7,6},{9,8},{10,9},{11,10},{13,12},{... | collective-permute-start | bytes 4616 | tf_op jit(solution)/shard_map/ppermute | solution.py:24
  9.2 3.0 %collective-permute-start.2 = (f32[3,8,8,2]{3,2,1,0:T(8,128)S(1)}, f32[3,8,8,2]{3,2,1,0:T(8,128)S(1)}, u32[]{:S(2)}, u32[]{:S(2)}) collective-permute-start(f32[3,8,8,2]{3,2,1,0:T(8,128)S(1)} %get-tuple-element.159), channel_id=1, source_target_pairs={{0,1},{1,2},{2,3},{4,5},{5,6},{6,7},{8,9},{9,10},{10,11},{12,13},{... | collective-permute-start | bytes 4616 | tf_op jit(solution)/shard_map/ppermute | solution.py:23
  12.3 0.7 constant_dynamic-slice_fusion.3
  13.0 0.6 copy-done.5
  13.7 0.0 copy-done.6
  13.7 0.1 multiply_bitcast_fusion.1
  13.8 0.7 constant_dynamic-slice_fusion.5
  14.5 1.3 %dynamic-slice.2 = f32[1,1]{1,0:T(1,128)} dynamic-slice(f32[4,256]{1,0:T(4,128)} %constant.188.clone, s32[]{:T(128)S(6)} %select_n.84, s32[]{:T(128)S(6)} %add.193), dynamic_slice_sizes={1,1} | dynamic-slice | bytes 12 | tf_op jit(solution)/shard_map/slice | solution.py:236
  15.7 0.6 dynamic-slice
  16.3 1.4 %bitcast_dynamic-update-slice_fusion = f32[4]{0:T(128)S(1)} fusion(f32[4]{0:T(128)S(1)} %broadcast.221.clone.1, u32[]{:T(128)} %bitcast.24, f32[4,256]{1,0:T(4,128)} %constant.190.clone, s32[]{:T(128)S(6)} %select_n.84), kind=kLoop, calls=%fused_computation.135 | loop fusion | bytes 28
  17.8 1.3 %bitcast_dynamic-update-slice_fusion.1 = f32[4]{0:T(128)S(1)} fusion(f32[4]{0:T(128)S(1)} %broadcast.221.clone, u32[]{:T(128)} %bitcast.24, f32[1,1]{1,0:T(1,128)} %dynamic-slice.2), kind=kLoop, calls=%fused_computation.136 | loop fusion | bytes 24
  19.1 6.9 %all-reduce.2 = (f32[4]{0:T(128)S(1)}, f32[4]{0:T(128)S(1)}) all-reduce(f32[4]{0:T(128)S(1)} %bitcast_dynamic-update-slice_fusion.1, f32[4]{0:T(128)S(1)} %bitcast_dynamic-update-slice_fusion), channel_id=4, replica_groups=mesh['circ'=8,'ax'=4] {'ax'}, use_global_device_ids=true, to_apply=%add | all-reduce | flops 8 | bytes 64
  26.0 0.1 copy.20
  26.1 0.1 copy.24
  26.2 0.0 copy-start.2
  26.2 0.4 multiply_bitcast_fusion
  26.6 0.3 copy-done.2
  26.9 0.4 convolution_bitcast_fusion.1
  27.4 31.0 %all-gather = f32[16,3,8,1,256]{4,2,3,1,0:T(8,128)S(1)} all-gather(f32[2,3,8,1,256]{4,2,3,1,0:T(8,128)S(1)} %copy.15), channel_id=2, replica_groups=mesh['circ'=8,'ax'=4] {'circ'}, dimensions={0}, use_global_device_ids=true | all-gather | bytes 442368 | tf_op jit(solution)/shard_map/all_gather | solution.py:195
  58.4 0.6 fusion.5
  59.0 0.0 copy-start.1
  59.1 0.0 copy-start.4
  59.1 0.7 copy-done.1
  59.7 0.0 copy-done.4
  59.7 0.5 convolution_bitcast_fusion
  60.3 31.0 %all-gather.1 = f32[16,3,8,1,256]{4,2,3,1,0:T(8,128)S(1)} all-gather(f32[2,3,8,1,256]{4,2,3,1,0:T(8,128)S(1)} %copy.16), channel_id=3, replica_groups=mesh['circ'=8,'ax'=4] {'circ'}, dimensions={0}, use_global_device_ids=true | all-gather | bytes 442368 | tf_op jit(solution)/shard_map/all_gather | solution.py:195
  91.3 0.6 fusion.3
  92.0 0.7 copy-done.3
  92.6 0.1 multiply_add_fusion
  92.8 0.8 slice_bitcast_fusion
  93.5 1.5 %fusion.11 = f32[3,8,8,256]{3,2,1,0:T(8,128)S(1)} fusion(f32[4,256,256]{2,1,0:T(8,128)} %constant.187.clone, s32[]{:T(128)S(6)} %select_n.84, f32[3,8,8,258]{3,2,1,0:T(8,128)S(1)} %constant_dynamic-update-slice_fusion.2, f32[3,8,8,256]{3,2,1,0:T(8,128)S(1)} %copy-done, f32[3,8,8,2]{3,2,1,0:T(8,128)S(1)} %collective-permute-done.2, ...), kind=kOutput, calls=%fused_computation.28 | convolution fusion | flops 152027136 | bytes 1148420 | tf_op jit(solution)/shard_map/fnck,jk->fncj/dot_general | solution.py:235
  95.1 0.1 slice.150
  95.2 0.2 copy.17
  95.4 5.2 %all-gather.3 = f32[12,8,8,1]{2,1,3,0:T(8,128)S(1)} all-gather(f32[3,8,8,1]{2,1,3,0:T(8,128)S(1)} %copy.17), channel_id=5, replica_groups=mesh['circ'=8,'ax'=4] {'ax'}, dimensions={0}, use_global_device_ids=true | all-gather | bytes 3840 | tf_op jit(solution)/shard_map/all_gather | solution.py:33
  100.6 1.4 %fusion.9 = f32[3,8,8,256]{3,2,1,0:T(8,128)S(1)} fusion(f32[4,256,256]{2,1,0:T(8,128)} %constant.189.clone, s32[]{:T(128)S(6)} %select_n.84, f32[3,8,8,256]{3,2,1,0:T(8,128)S(1)} %fusion.11, f32[256]{0:T(256)S(1)} %bitcast.82, f32[3,8,8]{2,1,0:T(8,128)S(1)} %get-tuple-element.131, f32[256]{0:T(256)S(1)} %bitcast.80), kind=kOutput, calls=%fused_computation.26 | convolution fusion | flops 151142400 | bytes 658180 | tf_op jit(solution)/shard_map/fnck,jk->fncj/dot_general | solution.py:238
  102.0 0.2 copy.18
  102.2 8.8 %all-gather.5 = f32[12,8,8,1]{2,1,3,0:T(8,128)S(1)} all-gather(f32[3,8,8,1]{2,1,3,0:T(8,128)S(1)} %copy.18), channel_id=7, replica_groups=mesh['circ'=8,'ax'=4] {'ax'}, dimensions={0}, use_global_device_ids=true | all-gather | bytes 3840 | tf_op jit(solution)/shard_map/all_gather | solution.py:33
  111.0 3.8 %while.27 = (s32[]{:T(128)}, f32[3,8,8]{2,1,0:T(8,128)S(1)}, s32[]{:T(128)}, f32[4,1,1,1]{0,3,2,1:T(1,128)S(1)}, f32[4,3,8,8]{3,2,1,0:T(8,128)S(1)}, /*index=5*/s32[]{:T(128)}, s32[]{:T(128)}, s32[]{:T(128)}, s32[]{:T(128)}) while((s32[]{:T(128)}, f32[3,8,8]{2,1,0:T(8,128)S(1)}, s32[]{:T(128)}, f32[4,1,1,1]{0,3,2,1:T(1,128)S(1)}, ...), condition=%wide.region_3.4_spmd, body=%wide.region_2.3_spmd.sunk | while | flops 390 | bytes 2471 | solution.py:42
  111.0 0.6 constant_dynamic-slice_fusion.9
  111.6 0.7 bitcast_add_fusion.5
  112.3 0.6 constant_dynamic-slice_fusion.9
  112.9 0.7 bitcast_add_fusion.5
  113.5 0.6 constant_dynamic-slice_fusion.9
  114.1 0.7 bitcast_add_fusion.5
  114.8 0.8 multiply_add_fusion.1
  (31 shorter events, 0.2 us)
Async XLA Ops:
  0.6 7.1 %copy-start = (f32[3,8,8,256]{3,2,1,0:T(8,128)S(1)}, f32[3,8,8,256]{3,2,1,0:T(8,128)}, u32[]{:S(2)}) copy-start(f32[3,8,8,256]{3,2,1,0:T(8,128)} %param.16) | copy-start | bytes 589828
  1.7 24.4 %collective-permute-start = (f32[3,8,5,256]{3,2,1,0:T(8,128)S(1)}, f32[3,8,5,256]{3,2,1,0:T(8,128)S(1)}, u32[]{:S(2)}, u32[]{:S(2)}) collective-permute-start(f32[3,8,5,256]{3,2,1,0:T(8,128)S(1)} %get-tuple-element.162), channel_id=1, source_target_pairs={{4,0},{8,4},{12,8},{16,12},{20,16},{24,20},{28,24},{0,28},{5,1},{9... | collective-permute-start | bytes 368648 | tf_op jit(solution)/shard_map/ppermute | solution.py:24
  7.8 18.4 %collective-permute-start.1 = (f32[3,8,5,256]{3,2,1,0:T(8,128)S(1)}, f32[3,8,5,256]{3,2,1,0:T(8,128)S(1)}, u32[]{:S(2)}, u32[]{:S(2)}) collective-permute-start(f32[3,8,5,256]{3,2,1,0:T(8,128)S(1)} %get-tuple-element.163), channel_id=1, source_target_pairs={{0,4},{4,8},{8,12},{12,16},{16,20},{20,24},{24,28},{28,0},{1,5},{5... | collective-permute-start | bytes 368648 | tf_op jit(solution)/shard_map/ppermute | solution.py:23
  7.9 85.7 %collective-permute-start.3 = (f32[3,8,8,2]{3,2,1,0:T(8,128)S(1)}, f32[3,8,8,2]{3,2,1,0:T(8,128)S(1)}, u32[]{:S(2)}, u32[]{:S(2)}) collective-permute-start(f32[3,8,8,2]{3,2,1,0:T(8,128)S(1)} %get-tuple-element.160), channel_id=1, source_target_pairs={{1,0},{2,1},{3,2},{5,4},{6,5},{7,6},{9,8},{10,9},{11,10},{13,12},{... | collective-permute-start | bytes 4616 | tf_op jit(solution)/shard_map/ppermute | solution.py:24
  9.2 84.4 %collective-permute-start.2 = (f32[3,8,8,2]{3,2,1,0:T(8,128)S(1)}, f32[3,8,8,2]{3,2,1,0:T(8,128)S(1)}, u32[]{:S(2)}, u32[]{:S(2)}) collective-permute-start(f32[3,8,8,2]{3,2,1,0:T(8,128)S(1)} %get-tuple-element.159), channel_id=1, source_target_pairs={{0,1},{1,2},{2,3},{4,5},{5,6},{6,7},{8,9},{9,10},{10,11},{12,13},{... | collective-permute-start | bytes 4616 | tf_op jit(solution)/shard_map/ppermute | solution.py:23
  13.0 0.7 copy-start.5
  13.0 0.7 copy-start.6
  14.5 1.3 %copy-start.7 = (u32[32]{0:T(128)S(1)}, u32[32]{0:T(128)}, u32[]{:S(2)}) copy-start(u32[32]{0:T(128)} %constant.194) | copy-start | bytes 388
  26.2 0.7 copy-start.2
  59.0 0.7 copy-start.1
  59.1 0.7 copy-start.4
  92.0 0.7 copy-start.3
where the time goes:
time: 116 us
  blocking collectives  82.8 us (71%)
  local copies, waits for them, and re-layouts  12.8 us (11%)
  starting transfers between devices  10.4 us (9%)
  matrix products  5.18 us (4%)
  other arithmetic  3.34 us (3%)
    all_gather x2, blocking collectives, circ_carry(): piece = lax.all_gather(state[None], 'circ', axis=0, tiled=True)  61.9 us
    all_gather x2, blocking collectives, entering_2(): gathered = jax.tree.map(lambda a: lax.all_gather(a, axis), part)  14 us
    ppermute x2, starting transfers between devices, with_halo(): after = lax.ppermute(initial, axis, down)  7.32 us
    unnamed x1, blocking collectives  6.9 us
    unnamed x22, local copies, waits for them, and re-layouts  5.69 us
    ppermute x2, starting transfers between devices, with_halo(): before = lax.ppermute(last, axis, up)  3.04 us
  transfers between devices with their start and end apart: 4, of which 0 were waited for; matrix products, arithmetic and copies ran while one was open for 9% of the time, Pallas kernels for 0%

commit v1 on v0

v1 whole, which is shorter than its diff:
```python
import functools
import math

import jax
import jax.numpy as jnp
import numpy as np
from jax import lax
from jax.experimental import pallas as pl
from jax.experimental.pallas import tpu as pltpu
from jax.sharding import PartitionSpec as P

ALPHA_DERIV = 1.0 / 3.0
ALPHA_FILTER = 0.4999
DERIV_NEAR = 14.0 / 9.0
DERIV_FAR = 1.0 / 9.0
HALO = 4
MESH = pl.DeviceIdType.MESH
PRECISE = lax.Precision.HIGHEST


def root_of(coupling):
    return (-1.0 + math.sqrt(1.0 - 4.0 * coupling * coupling)) / (2.0 * coupling)


def circ_parts():
    quotient = DERIV_FAR / (2.0 * ALPHA_DERIV)
    rem = DERIV_NEAR - quotient
    amp_deriv = -rem / (2.0 * ALPHA_DERIV)
    fir_deriv = np.zeros(2 * HALO + 1)
    fir_deriv[HALO + 1] = 0.5 * quotient
    fir_deriv[HALO - 1] = -0.5 * quotient
    scale = -(1.0 - 2.0 * ALPHA_FILTER)
    power = np.array([1.0])
    for _ in range(5):
        power = np.polymul(power, np.array([-0.5, 0.5]))
    poly, left = np.polydiv(power, np.array([2.0 * ALPHA_FILTER, 1.0]))
    waves = np.polynomial.chebyshev.poly2cheb(poly[::-1])
    fir_filter = np.zeros(2 * HALO + 1)
    fir_filter[HALO] = scale * waves[0]
    for step in range(1, HALO + 1):
        fir_filter[HALO + step] = fir_filter[HALO - step] = 0.5 * scale * waves[step]
    amp_filter = scale * left[-1] / math.sqrt(1.0 - 4.0 * ALPHA_FILTER**2)
    return (
        (root_of(ALPHA_DERIV), amp_deriv, -1.0, fir_deriv),
        (root_of(ALPHA_FILTER), amp_filter, 1.0, fir_filter),
    )


def circ_tables(lines, cells, peers):
    length = cells * peers
    parts = circ_parts()
    eye = np.eye(lines)
    steps = np.arange(cells)
    ends, local, halo, apply = [], [], [], []
    for root, amp, sign, fir in parts:
        gain = amp / (1.0 - root**length)
        block = np.zeros((cells, cells))
        before = np.zeros((cells, HALO))
        after = np.zeros((cells, HALO))
        for j in range(cells):
            for i in range(cells):
                k = (i - j) % length
                if k == 0:
                    block[j, i] = gain * (1.0 + root**length) if sign > 0 else 0.0
                else:
                    block[j, i] = gain * (root**k + sign * root ** (length - k))
                if abs(i - j) <= HALO:
                    block[j, i] += fir[HALO + i - j]
            for m in range(HALO):
                k = m - HALO - j
                if k >= -HALO:
                    before[j, m] = fir[HALO + k]
                k = cells + m - j
                if k <= HALO:
                    after[j, m] = fir[HALO + k]
        local.append(np.kron(eye, block))
        spread = []
        for side in (before, after):
            table = np.zeros((lines * cells, lines * HALO))
            for line in range(lines):
                base = 2 * HALO * (line % (lines // 2)) + HALO * (line // (lines // 2))
                table[line * cells : (line + 1) * cells, base : base + HALO] = side
            spread.append(table)
        halo.append(np.concatenate(spread, axis=1))
        ends.append(np.kron(eye, (root ** (cells - 1 - steps))[None, :]))
        ends.append(np.kron(eye, (root**steps)[None, :]))
        up = np.kron(eye, (sign * gain * root ** (steps + 1.0))[:, None])
        down = np.kron(eye, (gain * root ** (cells - steps * 1.0))[:, None])
        apply.append((up, down))
    nothing = np.zeros_like(apply[0][0])
    from_ends = np.concatenate(
        [
            np.concatenate([*apply[0], nothing, nothing], axis=1),
            np.concatenate([nothing, nothing, *apply[1]], axis=1),
        ],
        axis=0,
    )
    return (
        np.concatenate(ends, axis=0),
        np.concatenate(local, axis=0),
        np.concatenate(halo, axis=0),
        from_ends,
    )


def carry_weights(lines, cells, peers, halves, tiles):
    rows = lines // 8
    weights = np.zeros((tiles, peers))
    for half in range(halves):
        for kind in range(4):
            root = circ_parts()[kind // 2][0]
            for k in range(1, peers):
                gap = k - 1 if kind % 2 == 0 else peers - 1 - k
                first = half * 4 * rows + kind * rows
                weights[first : first + rows, k] = root ** (cells * gap)
    return weights


def axial_tables(cells, peers):
    length = cells * peers
    lower = np.full(length, ALPHA_DERIV)
    upper = np.full(length, ALPHA_DERIV)
    lower[[0, 1, length - 2, length - 1]] = 0.0, 0.25, 0.25, 2.0
    upper[[0, 1, length - 2, length - 1]] = 2.0, 0.25, 0.25, 0.0
    ahead = np.ones(length)
    behind = np.ones(length)
    for i in range(1, length):
        ahead[i] = 1.0 - lower[i] * upper[i - 1] / ahead[i - 1]
    for i in range(length - 2, -1, -1):
        behind[i] = 1.0 - upper[i] * lower[i + 1] / behind[i + 1]
    grow = -lower / behind
    back = -upper / ahead
    inverse = np.diag(1.0 / (ahead + behind - 1.0))
    for i in range(1, length):
        inverse[i, :i] = grow[i] * inverse[i - 1, :i]
    for i in range(length - 2, -1, -1):
        inverse[i, i + 1 :] = back[i] * inverse[i + 1, i + 1 :]
    right = np.zeros((length, length))
    for k in range(2, length - 2):
        right[k, [k - 2, k - 1, k + 1, k + 2]] = (
            -0.25 * DERIV_FAR,
            -0.5 * DERIV_NEAR,
            0.5 * DERIV_NEAR,
            0.25 * DERIV_FAR,
        )
    right[0, :3] = -2.5, 2.0, 0.5
    right[1, [0, 2]] = -0.75, 0.75
    right[length - 2, [length - 3, length - 1]] = -0.75, 0.75
    right[length - 1, length - 3 :] = -0.5, -2.0, 2.5
    whole = np.zeros((length, length))
    for k in range(length):
        for j in np.nonzero(right[k])[0]:
            whole[:, j] += inverse[:, k] * right[k, j]

    own = np.zeros((peers, cells, cells))
    ends = np.zeros((peers, 8, cells))
    apply = np.zeros((peers, peers, 8, cells))
    for p in range(peers):
        start, stop = p * cells, (p + 1) * cells
        own[p] = whole[start:stop, start:stop].T
        if p < peers - 1:
            ends[p, 0] = whole[stop, start:stop]
            ends[p, 0, -1] = whole[stop + 1, stop - 1] / grow[stop + 1]
            ends[p, 1, -1] = 1.0
        if p > 0:
            ends[p, 2] = whole[start - 1, start:stop]
            ends[p, 2, 0] = whole[start - 2, start] / back[start - 2]
            ends[p, 3, 0] = 1.0
        forward = np.concatenate([[1.0], np.cumprod(grow[start + 1 : stop])])
        reverse = np.concatenate([np.cumprod(back[start : stop - 1][::-1])[::-1], [1.0]])
        for q in range(peers):
            if q < p:
                apply[p, q, 0] = forward * np.prod(grow[(q + 1) * cells + 1 : start + 1])
            if q == p - 1:
                apply[p, q, 1, 0] = (
                    whole[start, start - 1] - whole[start + 1, start - 1] / grow[start + 1]
                )
            if q > p:
                apply[p, q, 2] = reverse * np.prod(back[stop - 1 : q * cells - 1])
            if q == p + 1:
                apply[p, q, 3, -1] = (
                    whole[stop - 1, stop] - whole[stop - 2, stop] / back[stop - 2]
                )
    return own, ends, apply.reshape(peers, peers * 8, cells)


def dot(left, right, dims=((1,), (0,))):
    return lax.dot_general(
        left, right, (dims, ((), ())), precision=PRECISE, preferred_element_type=jnp.float32
    )


def kernel(
    sizes,
    fields_hbm,
    ends_hbm,
    local_hbm,
    halo_hbm,
    apply_hbm,
    own_hbm,
    ax_ends_hbm,
    ax_apply_hbm,
    weights,
    deriv_ref,
    axial_ref,
    filter_ref,
    fields,
    ends_table,
    local_table,
    halo_table,
    apply_table,
    own_table,
    ax_ends_table,
    ax_apply_table,
    outgoing,
    gathered,
    combined,
    incoming,
    halo_out,
    halo_in,
    ax_out,
    ax_in,
    load_sems,
    gather_send,
    gather_recv,
    return_send,
    return_recv,
    halo_send,
    halo_recv,
    ax_send,
    ax_recv,
):
    peers, ax_peers, lines, cells, width, chunk = sizes
    here = lax.axis_index("circ")
    place = lax.axis_index("ax")
    halves = width // 128
    row_blocks = 4 * lines // 8
    others = [lax.rem(here + k, peers) for k in range(peers)]
    ax_others = [lax.rem(place + k, ax_peers) for k in range(ax_peers)]

    loads = [
        pltpu.make_async_copy(source, target, load_sems.at[i])
        for i, (source, target) in enumerate(
            (
                (fields_hbm, fields),
                (ends_hbm, ends_table),
                (ax_ends_hbm.at[place], ax_ends_table),
                (local_hbm, local_table),
                (own_hbm.at[place], own_table),
                (halo_hbm, halo_table),
                (ax_apply_hbm.at[place], ax_apply_table),
                (apply_hbm, apply_table),
            )
        )
    ]
    for load in loads:
        load.start()

    barrier = pltpu.get_barrier_semaphore()
    for k in range(1, peers):
        pl.semaphore_signal(barrier, inc=1, device_id={"circ": others[k]}, device_id_type=MESH)
    for k in range(1, ax_peers):
        pl.semaphore_signal(barrier, inc=1, device_id={"ax": ax_others[k]}, device_id_type=MESH)

    loads[0].wait()
    loads[1].wait()
    block = fields[...]
    flat = block.reshape(lines * cells, width)
    end_sums = dot(ends_table[...], flat)
    for half in range(halves):
        outgoing[half * row_blocks : (half + 1) * row_blocks] = end_sums[
            :, half * 128 : (half + 1) * 128
        ].reshape(row_blocks, 8, 128)
    if halves * row_blocks < peers * chunk:
        outgoing[halves * row_blocks :] = jnp.zeros(
            (peers * chunk - halves * row_blocks, 8, 128), jnp.float32
        )

    pl.semaphore_wait(barrier, peers - 1 + ax_peers - 1)

    gathers = []
    for k in range(1, peers):
        copy = pltpu.make_async_remote_copy(
            src_ref=outgoing.at[pl.ds(others[k] * chunk, chunk)],
            dst_ref=gathered.at[here],
            send_sem=gather_send.at[k],
            recv_sem=gather_recv.at[here],
            device_id={"circ": others[k]},
            device_id_type=MESH,
        )
        copy.start()
        gathers.append(copy)

    loads[2].wait()
    ax_sums = dot(ax_ends_table[...], flat, ((1,), (1,)))
    ax_out[...] = ax_sums
    ax_in[place] = ax_sums
    ax_copies = []
    for k in range(1, ax_peers):
        copy = pltpu.make_async_remote_copy(
            src_ref=ax_out,
            dst_ref=ax_in.at[place],
            send_sem=ax_send.at[k],
            recv_sem=ax_recv.at[place],
            device_id={"ax": ax_others[k]},
            device_id_type=MESH,
        )
        copy.start()
        ax_copies.append(copy)

    half_lines = lines // 2
    last = block[:, cells - 8 :, :]
    initial = block[:, :8, :]
    row = lax.broadcasted_iota(jnp.int32, (half_lines, 8, width), 1)
    halo_out[0] = jnp.where(row < HALO, pltpu.roll(last[:half_lines], HALO, 1), last[half_lines:])
    halo_out[1] = jnp.where(
        row < HALO, initial[:half_lines], pltpu.roll(initial[half_lines:], HALO, 1)
    )
    halos = []
    for side, target in ((0, others[1]), (1, others[peers - 1])):
        copy = pltpu.make_async_remote_copy(
            src_ref=halo_out.at[side],
            dst_ref=halo_in.at[side],
            send_sem=halo_send.at[side],
            recv_sem=halo_recv.at[side],
            device_id={"circ": target},
            device_id_type=MESH,
        )
        copy.start()
        halos.append(copy)

    loads[3].wait()
    rows = lines * cells
    own_part = dot(local_table[...], flat)
    deriv_ref[...] = own_part[:rows].reshape(lines, cells, width)
    filter_ref[...] = block + own_part[rows:].reshape(lines, cells, width)

    for k in range(1, peers):
        source = others[k]
        pltpu.make_async_remote_copy(
            src_ref=gathered.at[source],
            dst_ref=gathered.at[source],
            send_sem=gather_send.at[k],
            recv_sem=gather_recv.at[source],
            device_id={"circ": source},
            device_id_type=MESH,
        ).wait_recv()
    gathered[here] = outgoing[pl.ds(here * chunk, chunk)]
    factors = [
        [weights[(here * chunk + tile) * peers + k] for k in range(peers)] for tile in range(chunk)
    ]
    returns = []
    for k in range(peers):
        for tile in range(chunk):
            total = None
            for j in range(peers):
                if j == k:
                    continue
                term = factors[tile][(k - j) % peers] * gathered[others[j], tile]
                total = term if total is None else total + term
            if k == 0:
                incoming[here * chunk + tile] = total
            else:
                combined[k, tile] = total
        if k == 0:
            continue
        copy = pltpu.make_async_remote_copy(
            src_ref=combined.at[k],
            dst_ref=incoming.at[pl.ds(here * chunk, chunk)],
            send_sem=return_send.at[k],
            recv_sem=return_recv.at[here],
            device_id={"circ": others[k]},
            device_id_type=MESH,
        )
        copy.start()
        returns.append(copy)

    loads[4].wait()
    axial = dot(flat, own_table[...])
    loads[6].wait()
    for k in range(1, ax_peers):
        source = ax_others[k]
        pltpu.make_async_remote_copy(
            src_ref=ax_out,
            dst_ref=ax_in.at[source],
            send_sem=ax_send.at[k],
            recv_sem=ax_recv.at[source],
            device_id={"ax": source},
            device_id_type=MESH,
        ).wait_recv()
    received = ax_in[...].reshape(ax_peers * 8, rows)
    axial = axial + dot(received, ax_apply_table[...], ((0,), (0,)))
    axial_ref[...] = axial.reshape(lines, cells, width)

    loads[5].wait()
    for copy in halos:
        copy.wait_recv()
    edge = dot(halo_table[...], halo_in[...].reshape(2 * lines * HALO, width))
    deriv_ref[...] += edge[:rows].reshape(lines, cells, width)
    filter_ref[...] += edge[rows:].reshape(lines, cells, width)

    loads[7].wait()
    for k in range(1, peers):
        source = others[k]
        pltpu.make_async_remote_copy(
            src_ref=combined.at[k],
            dst_ref=incoming.at[pl.ds(source * chunk, chunk)],
            send_sem=return_send.at[k],
            recv_sem=return_recv.at[source],
            device_id={"circ": source},
            device_id_type=MESH,
        ).wait_recv()
    entering = jnp.concatenate(
        [
            incoming[half * row_blocks : (half + 1) * row_blocks].reshape(row_blocks * 8, 128)
            for half in range(halves)
        ],
        axis=1,
    )
    carried = dot(apply_table[...], entering)
    deriv_ref[...] += carried[:rows].reshape(lines, cells, width)
    filter_ref[...] += carried[rows:].reshape(lines, cells, width)

    for copy in gathers + ax_copies + halos + returns:
        copy.wait_send()


def shards(fields):
    peers, ax_peers = lax.axis_size("circ"), lax.axis_size("ax")
    components, radial, cells, width = fields.shape
    lines = components * radial
    halves = width // 128
    tiles = halves * 4 * lines // 8
    chunk = -(-tiles // peers)
    tables = list(circ_tables(lines, cells, peers)) + list(axial_tables(width, ax_peers))
    weights = carry_weights(lines, cells, peers, halves, peers * chunk).reshape(-1)
    tables = [jnp.asarray(table, jnp.float32) for table in tables]
    out = jax.ShapeDtypeStruct((lines, cells, width), jnp.float32)
    scratch = [
        pltpu.VMEM((lines, cells, width), jnp.float32),
        pltpu.VMEM(tables[0].shape, jnp.float32),
        pltpu.VMEM(tables[1].shape, jnp.float32),
        pltpu.VMEM(tables[2].shape, jnp.float32),
        pltpu.VMEM(tables[3].shape, jnp.float32),
        pltpu.VMEM(tables[4].shape[1:], jnp.float32),
        pltpu.VMEM(tables[5].shape[1:], jnp.float32),
        pltpu.VMEM(tables[6].shape[1:], jnp.float32),
        pltpu.VMEM((peers * chunk, 8, 128), jnp.float32),
        pltpu.VMEM((peers, chunk, 8, 128), jnp.float32),
        pltpu.VMEM((peers, chunk, 8, 128), jnp.float32),
        pltpu.VMEM((peers * chunk, 8, 128), jnp.float32),
        pltpu.VMEM((2, lines // 2, 8, width), jnp.float32),
        pltpu.VMEM((2, lines // 2, 8, width), jnp.float32),
        pltpu.VMEM((8, lines * cells), jnp.float32),
        pltpu.VMEM((ax_peers, 8, lines * cells), jnp.float32),
        pltpu.SemaphoreType.DMA((8,)),
        pltpu.SemaphoreType.DMA((peers,)),
        pltpu.SemaphoreType.DMA((peers,)),
        pltpu.SemaphoreType.DMA((peers,)),
        pltpu.SemaphoreType.DMA((peers,)),
        pltpu.SemaphoreType.DMA((2,)),
        pltpu.SemaphoreType.DMA((2,)),
        pltpu.SemaphoreType.DMA((ax_peers,)),
        pltpu.SemaphoreType.DMA((ax_peers,)),
    ]
    results = pl.pallas_call(
        functools.partial(kernel, (peers, ax_peers, lines, cells, width, chunk)),
        out_shape=(out, out, out),
        in_specs=[pl.BlockSpec(memory_space=pl.ANY)] * 8
        + [pl.BlockSpec(memory_space=pltpu.SMEM)],
        out_specs=[pl.BlockSpec(memory_space=pltpu.VMEM)] * 3,
        scratch_shapes=scratch,
        compiler_params=pltpu.CompilerParams(
            collective_id=0, has_side_effects=True, vmem_limit_bytes=32 * 1024 * 1024
        ),
    )(fields.reshape(lines, cells, width), *tables, jnp.asarray(weights, jnp.float32))
    return tuple(result.reshape(fields.shape) for result in results)


def solution(mesh):
    placed = P(None, None, "circ", "ax")
    return jax.shard_map(
        shards, mesh=mesh, in_specs=(placed,), out_specs=(placed,) * 3, check_vma=False
    )
```

time: 116 us -> 31.8 us (0.27)
  blocking collectives: 82.8 us -> 0 us
  Pallas kernels: 0 us -> 20.4 us
  starting transfers between devices: 10.4 us -> 0 us
  matrix products: 5.18 us -> 0 us
  other arithmetic: 3.34 us -> 0 us
  local copies, waits for them, and re-layouts: 12.8 us -> 10.3 us
    all_gather x4 -> x0, blocking collectives: 76 us -> none  [the longest x2 61.9 us: circ_carry(): piece = lax.all_gather(state[None], 'circ', axis=0, tiled=True)]
    pallas_call x0 -> x1, Pallas kernels: none -> 20.4 us  [shards(): pl.pallas_call(functools.partial(kernel, (peers, ax_peers, lines, cells,...]
    ppermute x4 -> x0, starting transfers between devices: 10.4 us -> none  [the longest x2 7.32 us: with_halo(): after = lax.ppermute(initial, axis, down)]
    unnamed x1 -> x0, blocking collectives: 6.9 us -> none
    dot_general x6 -> x0, matrix products: 5.18 us -> none  [the longest x1 1.54 us: shards(): jnp.einsum('fnck,jk->fncj', axial_right, fwd_block, precision=PRECISE)]
    unnamed x22 -> x21, local copies, waits for them, and re-layouts: 5.69 us -> 10.3 us
    dynamic_slice x5 -> x0, local copies, waits for them, and re-layouts: 3.16 us -> none  [the longest x3 1.75 us: one(): lax.dynamic_index_in_dim(a, source, 0, False)]
    slice x11 -> x0, local copies, waits for them, and re-layouts: 3.03 us -> none  [the longest x1 1.28 us: shards(): fwd_grow[-1].reshape(1, 1, 1)]
  transfers between devices with their start and end apart: 4 -> 0, of which waited for: 0 -> 0; matrix products, arithmetic and copies ran while one was open for 9% -> 0% of each run, Pallas kernels for 0% -> 0%
where the time goes in v1:
time: 31.8 us; the launch traced here: 31.4 us
  Pallas kernels  20.4 us (64%)
  local copies, waits for them, and re-layouts  10.3 us (32%)
  between operations  0.66 us (2%)
    pallas_call x1, Pallas kernels, shards(): pl.pallas_call(functools.partial(kernel, (peers, ax_peers, lines, cells,...  20.4 us
    unnamed x21, local copies, waits for them, and re-layouts  10.3 us

profile of v1, /device:TPU:0, one launch (start us, length us, event | category | flops | bytes accessed | tf_op | source)
XLA Modules:
  0.0 31.4 jit_solution(2869165527949509843)
XLA Ops:
  0.6 0.0 copy-start.8
  0.6 0.7 %copy-done.8 = f32[192]{0:T(256)S(1)} copy-done((f32[192]{0:T(256)S(1)}, f32[192]{0:T(256)}, u32[]{:S(2)}) %copy-start.8) | copy-done | bytes 792
  1.3 0.0 copy-start
  1.3 1.2 %copy-done = f32[4,256,256]{2,1,0:T(8,128)S(1)} copy-done((f32[4,256,256]{2,1,0:T(8,128)S(1)}, f32[4,256,256]{2,1,0:T(8,128)}, u32[]{:S(2)}) %copy-start) | copy-done | bytes 1048600
  2.5 0.0 copy-start.1
  2.5 1.0 %copy-done.1 = f32[384,192]{1,0:T(8,128)S(1)} copy-done((f32[384,192]{1,0:T(8,128)S(1)}, f32[384,192]{1,0:T(8,128)}, u32[]{:S(2)}) %copy-start.1) | copy-done | bytes 294936
  3.5 0.0 copy-start.2
  3.5 1.0 %copy-done.2 = f32[384,192]{1,0:T(8,128)S(1)} copy-done((f32[384,192]{1,0:T(8,128)S(1)}, f32[384,192]{1,0:T(8,128)}, u32[]{:S(2)}) %copy-start.2) | copy-done | bytes 294936
  4.5 0.0 copy-start.3
  4.5 0.9 %copy-done.3 = f32[3,8,8,256]{3,2,1,0:T(8,128)S(1)} copy-done((f32[3,8,8,256]{3,2,1,0:T(8,128)S(1)}, f32[3,8,8,256]{3,2,1,0:T(8,128)}, u32[]{:S(2)}) %copy-start.3) | copy-done | bytes 196632
  5.5 0.0 copy-start.4
  5.5 0.9 %copy-done.4 = f32[384,96]{1,0:T(8,128)S(1)} copy-done((f32[384,96]{1,0:T(8,128)S(1)}, f32[384,96]{1,0:T(8,128)}, u32[]{:S(2)}) %copy-start.4) | copy-done | bytes 147480
  6.4 0.0 copy-start.5
  6.4 0.9 %copy-done.5 = f32[4,32,256]{2,1,0:T(8,128)S(1)} copy-done((f32[4,32,256]{2,1,0:T(8,128)S(1)}, f32[4,32,256]{2,1,0:T(8,128)}, u32[]{:S(2)}) %copy-start.5) | copy-done | bytes 131096
  7.3 0.0 copy-start.6
  7.3 0.9 %copy-done.6 = f32[96,192]{1,0:T(8,128)S(1)} copy-done((f32[96,192]{1,0:T(8,128)S(1)}, f32[96,192]{1,0:T(8,128)}, u32[]{:S(2)}) %copy-start.6) | copy-done | bytes 73752
  8.2 0.0 copy-start.7
  8.2 0.8 %copy-done.7 = f32[4,8,256]{2,1,0:T(8,128)S(1)} copy-done((f32[4,8,256]{2,1,0:T(8,128)S(1)}, f32[4,8,256]{2,1,0:T(8,128)}, u32[]{:S(2)}) %copy-start.7) | copy-done | bytes 32792
  8.9 20.4 %shard_map.112 = (f32[24,8,256]{2,1,0:T(8,128)S(1)}, f32[24,8,256]{2,1,0:T(8,128)S(1)}, f32[24,8,256]{2,1,0:T(8,128)S(1)}) custom-call(f32[24,8,256]{2,1,0:T(8,128)S(1)} %bitcast.4, f32[96,192]{1,0:T(8,128)S(1)} %copy-done.6, f32[384,192]{1,0:T(8,128)S(1)} %copy-done.2, f32[384,192]{1,0:T(8,128)S(1)} %copy-done.1, f32[384,96]{1,0:T(8,128)S(1)} %copy-done.4, ...), custom_call_target="tpu_custom_call" | custom-call | tf_op jit(solution)/shard_map/pallas_call | solution.py:466
  29.4 0.7 %copy.15 = f32[3,8,8,256]{3,2,1,0:T(8,128)} copy(f32[3,8,8,256]{3,2,1,0:T(8,128)S(1)} %bitcast.7) | data formatting | bytes 393216
  30.0 0.7 %copy.16 = f32[3,8,8,256]{3,2,1,0:T(8,128)} copy(f32[3,8,8,256]{3,2,1,0:T(8,128)S(1)} %bitcast.6) | data formatting | bytes 393216
  30.7 0.7 %copy.17 = f32[3,8,8,256]{3,2,1,0:T(8,128)} copy(f32[3,8,8,256]{3,2,1,0:T(8,128)S(1)} %bitcast.5) | data formatting | bytes 393216
Async XLA Ops:
  0.6 0.7 %copy-start.8 = (f32[192]{0:T(256)S(1)}, f32[192]{0:T(256)}, u32[]{:S(2)}) copy-start(f32[192]{0:T(256)} %constant.23.clone.weights) | copy-start | bytes 2308
  1.3 1.2 %copy-start = (f32[4,256,256]{2,1,0:T(8,128)S(1)}, f32[4,256,256]{2,1,0:T(8,128)}, u32[]{:S(2)}) copy-start(f32[4,256,256]{2,1,0:T(8,128)} %constant.20.clone.own_hbm) | copy-start | bytes 3145732
  2.5 1.0 %copy-start.1 = (f32[384,192]{1,0:T(8,128)S(1)}, f32[384,192]{1,0:T(8,128)}, u32[]{:S(2)}) copy-start(f32[384,192]{1,0:T(8,128)} %constant.18.clone.halo_hbm) | copy-start | bytes 884740
  3.5 1.0 %copy-start.2 = (f32[384,192]{1,0:T(8,128)S(1)}, f32[384,192]{1,0:T(8,128)}, u32[]{:S(2)}) copy-start(f32[384,192]{1,0:T(8,128)} %constant.17.clone.local_hbm) | copy-start | bytes 884740
  4.5 0.9 %copy-start.3 = (f32[3,8,8,256]{3,2,1,0:T(8,128)S(1)}, f32[3,8,8,256]{3,2,1,0:T(8,128)}, u32[]{:S(2)}) copy-start(f32[3,8,8,256]{3,2,1,0:T(8,128)} %param.9) | copy-start | bytes 589828
  5.5 0.9 %copy-start.4 = (f32[384,96]{1,0:T(8,128)S(1)}, f32[384,96]{1,0:T(8,128)}, u32[]{:S(2)}) copy-start(f32[384,96]{1,0:T(8,128)} %constant.19.clone.apply_hbm) | copy-start | bytes 442372
  6.4 0.9 %copy-start.5 = (f32[4,32,256]{2,1,0:T(8,128)S(1)}, f32[4,32,256]{2,1,0:T(8,128)}, u32[]{:S(2)}) copy-start(f32[4,32,256]{2,1,0:T(8,128)} %constant.22.clone.ax_apply_hbm) | copy-start | bytes 393220
  7.3 0.9 %copy-start.6 = (f32[96,192]{1,0:T(8,128)S(1)}, f32[96,192]{1,0:T(8,128)}, u32[]{:S(2)}) copy-start(f32[96,192]{1,0:T(8,128)} %constant.16.clone.ends_hbm) | copy-start | bytes 221188
  8.2 0.8 %copy-start.7 = (f32[4,8,256]{2,1,0:T(8,128)S(1)}, f32[4,8,256]{2,1,0:T(8,128)}, u32[]{:S(2)}) copy-start(f32[4,8,256]{2,1,0:T(8,128)} %constant.21.clone.ax_ends_hbm) | copy-start | bytes 98308

commit v2 on v1

--- a/solution.py
+++ b/solution.py
@@ -103,17 +103,11 @@
     )
 
 
-def carry_weights(lines, cells, peers, halves, tiles):
-    rows = lines // 8
-    weights = np.zeros((tiles, peers))
-    for half in range(halves):
-        for kind in range(4):
-            root = circ_parts()[kind // 2][0]
-            for k in range(1, peers):
-                gap = k - 1 if kind % 2 == 0 else peers - 1 - k
-                first = half * 4 * rows + kind * rows
-                weights[first : first + rows, k] = root ** (cells * gap)
-    return weights
+def carry_factor(kind, gap_up, gap_down, cells):
+    deriv, filt = (root_of(ALPHA_DERIV) ** cells, root_of(ALPHA_FILTER) ** cells)
+    factor = jnp.where(kind == 0, jnp.float32(deriv**gap_up), jnp.float32(deriv**gap_down))
+    factor = jnp.where(kind == 2, jnp.float32(filt**gap_up), factor)
+    return jnp.where(kind == 3, jnp.float32(filt**gap_down), factor)
 
 
 def axial_tables(cells, peers):
@@ -184,7 +178,34 @@
     return own, ends, apply.reshape(peers, peers * 8, cells)
 
 
+def two_parts(value):
+    high = value.astype(jnp.bfloat16)
+    low = (value - high.astype(jnp.float32)).astype(jnp.bfloat16)
+    return high, low
+
+
+def padded_table(table):
+    return jnp.asarray(np.pad(table, ((0, 0), (0, -table.shape[1] % 128))), jnp.float32)
+
+
+def table_parts(value, axis):
+    high, low = two_parts(value)
+    return jnp.concatenate([high, high, low], axis=axis)
+
+
+def data_parts(value, axis):
+    if axis == 0 and value.shape[0] % 128:
+        filler = jnp.zeros((-value.shape[0] % 128, value.shape[1]), value.dtype)
+        value = jnp.concatenate([value, filler], axis=0)
+    high, low = two_parts(value)
+    return jnp.concatenate([high, low, high], axis=axis)
+
+
 def dot(left, right, dims=((1,), (0,))):
+    return lax.dot_general(left, right, (dims, ((), ())), preferred_element_type=jnp.float32)
+
+
+def precise_dot(left, right, dims):
     return lax.dot_general(
         left, right, (dims, ((), ())), precision=PRECISE, preferred_element_type=jnp.float32
     )
@@ -200,7 +221,6 @@
     own_hbm,
     ax_ends_hbm,
     ax_apply_hbm,
-    weights,
     deriv_ref,
     axial_ref,
     filter_ref,
@@ -266,7 +286,8 @@
     loads[1].wait()
     block = fields[...]
     flat = block.reshape(lines * cells, width)
-    end_sums = dot(ends_table[...], flat)
+    tall = data_parts(flat, 0)
+    end_sums = dot(table_parts(ends_table[...], 1), tall)
     for half in range(halves):
         outgoing[half * row_blocks : (half + 1) * row_blocks] = end_sums[
             :, half * 128 : (half + 1) * 128
@@ -291,8 +312,29 @@
         copy.start()
         gathers.append(copy)
 
+    half_lines = lines // 2
+    last = block[:, cells - 8 :, :]
+    initial = block[:, :8, :]
+    row = lax.broadcasted_iota(jnp.int32, (half_lines, 8, width), 1)
+    halo_out[0] = jnp.where(row < HALO, pltpu.roll(last[:half_lines], HALO, 1), last[half_lines:])
+    halo_out[1] = jnp.where(
+        row < HALO, initial[:half_lines], pltpu.roll(initial[half_lines:], HALO, 1)
+    )
+    halos = []
+    for side, target in ((0, others[1]), (1, others[peers - 1])):
+        copy = pltpu.make_async_remote_copy(
+            src_ref=halo_out.at[side],
+            dst_ref=halo_in.at[side],
+            send_sem=halo_send.at[side],
+            recv_sem=halo_recv.at[side],
+            device_id={"circ": target},
+            device_id_type=MESH,
+        )
+        copy.start()
+        halos.append(copy)
+
     loads[2].wait()
-    ax_sums = dot(ax_ends_table[...], flat, ((1,), (1,)))
+    ax_sums = precise_dot(ax_ends_table[...], flat, ((1,), (1,)))
     ax_out[...] = ax_sums
     ax_in[place] = ax_sums
     ax_copies = []
@@ -308,30 +350,9 @@
         copy.start()
         ax_copies.append(copy)
 
-    half_lines = lines // 2
-    last = block[:, cells - 8 :, :]
-    initial = block[:, :8, :]
-    row = lax.broadcasted_iota(jnp.int32, (half_lines, 8, width), 1)
-    halo_out[0] = jnp.where(row < HALO, pltpu.roll(last[:half_lines], HALO, 1), last[half_lines:])
-    halo_out[1] = jnp.where(
-        row < HALO, initial[:half_lines], pltpu.roll(initial[half_lines:], HALO, 1)
-    )
-    halos = []
-    for side, target in ((0, others[1]), (1, others[peers - 1])):
-        copy = pltpu.make_async_remote_copy(
-            src_ref=halo_out.at[side],
-            dst_ref=halo_in.at[side],
-            send_sem=halo_send.at[side],
-            recv_sem=halo_recv.at[side],
-            device_id={"circ": target},
-            device_id_type=MESH,
-        )
-        copy.start()
-        halos.append(copy)
-
     loads[3].wait()
     rows = lines * cells
-    own_part = dot(local_table[...], flat)
+    own_part = dot(table_parts(local_table[...], 1), tall)
     deriv_ref[...] = own_part[:rows].reshape(lines, cells, width)
     filter_ref[...] = block + own_part[rows:].reshape(lines, cells, width)
 
@@ -346,8 +367,13 @@
             device_id_type=MESH,
         ).wait_recv()
     gathered[here] = outgoing[pl.ds(here * chunk, chunk)]
+    kind_tiles = lines // 8
+    kinds = [
+        lax.rem(here * chunk + tile, row_blocks) // kind_tiles for tile in range(chunk)
+    ]
     factors = [
-        [weights[(here * chunk + tile) * peers + k] for k in range(peers)] for tile in range(chunk)
+        [carry_factor(kind, (k - 1) % peers, peers - 1 - k, cells) for k in range(peers)]
+        for kind in kinds
     ]
     returns = []
     for k in range(peers):
@@ -376,7 +402,7 @@
         returns.append(copy)
 
     loads[4].wait()
-    axial = dot(flat, own_table[...])
+    axial = dot(data_parts(flat, 1), table_parts(own_table[...], 0))
     loads[6].wait()
     for k in range(1, ax_peers):
         source = ax_others[k]
@@ -389,13 +415,13 @@
             device_id_type=MESH,
         ).wait_recv()
     received = ax_in[...].reshape(ax_peers * 8, rows)
-    axial = axial + dot(received, ax_apply_table[...], ((0,), (0,)))
+    axial = axial + precise_dot(received, ax_apply_table[...], ((0,), (0,)))
     axial_ref[...] = axial.reshape(lines, cells, width)
 
     loads[5].wait()
     for copy in halos:
         copy.wait_recv()
-    edge = dot(halo_table[...], halo_in[...].reshape(2 * lines * HALO, width))
+    edge = dot(table_parts(halo_table[...], 1), data_parts(halo_in[...].reshape(2 * lines * HALO, width), 0))
     deriv_ref[...] += edge[:rows].reshape(lines, cells, width)
     filter_ref[...] += edge[rows:].reshape(lines, cells, width)
 
@@ -417,7 +443,7 @@
         ],
         axis=1,
     )
-    carried = dot(apply_table[...], entering)
+    carried = dot(table_parts(apply_table[...], 1), data_parts(entering, 0))
     deriv_ref[...] += carried[:rows].reshape(lines, cells, width)
     filter_ref[...] += carried[rows:].reshape(lines, cells, width)
 
@@ -432,19 +458,14 @@
     halves = width // 128
     tiles = halves * 4 * lines // 8
     chunk = -(-tiles // peers)
-    tables = list(circ_tables(lines, cells, peers)) + list(axial_tables(width, ax_peers))
-    weights = carry_weights(lines, cells, peers, halves, peers * chunk).reshape(-1)
-    tables = [jnp.asarray(table, jnp.float32) for table in tables]
+    tables = [padded_table(table) for table in circ_tables(lines, cells, peers)]
+    own, ax_ends, ax_apply = axial_tables(width, ax_peers)
+    tables += [jnp.asarray(table, jnp.float32) for table in (own, ax_ends, ax_apply)]
     out = jax.ShapeDtypeStruct((lines, cells, width), jnp.float32)
     scratch = [
         pltpu.VMEM((lines, cells, width), jnp.float32),
-        pltpu.VMEM(tables[0].shape, jnp.float32),
-        pltpu.VMEM(tables[1].shape, jnp.float32),
-        pltpu.VMEM(tables[2].shape, jnp.float32),
-        pltpu.VMEM(tables[3].shape, jnp.float32),
-        pltpu.VMEM(tables[4].shape[1:], jnp.float32),
-        pltpu.VMEM(tables[5].shape[1:], jnp.float32),
-        pltpu.VMEM(tables[6].shape[1:], jnp.float32),
+        *[pltpu.VMEM(table.shape, table.dtype) for table in tables[:4]],
+        *[pltpu.VMEM(table.shape[1:], table.dtype) for table in tables[4:]],
         pltpu.VMEM((peers * chunk, 8, 128), jnp.float32),
         pltpu.VMEM((peers, chunk, 8, 128), jnp.float32),
         pltpu.VMEM((peers, chunk, 8, 128), jnp.float32),
@@ -466,14 +487,13 @@
     results = pl.pallas_call(
         functools.partial(kernel, (peers, ax_peers, lines, cells, width, chunk)),
         out_shape=(out, out, out),
-        in_specs=[pl.BlockSpec(memory_space=pl.ANY)] * 8
-        + [pl.BlockSpec(memory_space=pltpu.SMEM)],
+        in_specs=[pl.BlockSpec(memory_space=pltpu.HBM)] * 8,
         out_specs=[pl.BlockSpec(memory_space=pltpu.VMEM)] * 3,
         scratch_shapes=scratch,
         compiler_params=pltpu.CompilerParams(
-            collective_id=0, has_side_effects=True, vmem_limit_bytes=32 * 1024 * 1024
+            collective_id=0, has_side_effects=True, vmem_limit_bytes=60 * 1024 * 1024
         ),
-    )(fields.reshape(lines, cells, width), *tables, jnp.asarray(weights, jnp.float32))
+    )(fields.reshape(lines, cells, width), *tables)
     return tuple(result.reshape(fields.shape) for result in results)
 
 

time: 31.8 us -> 23.4 us (0.74)
  local copies, waits for them, and re-layouts: 10.3 us -> 3.33 us
  Pallas kernels: 20.4 us -> 19.3 us
    unnamed x21 -> x7, local copies, waits for them, and re-layouts: 10.3 us -> 3.33 us
    pallas_call x1, Pallas kernels: 20.4 us -> 19.3 us  [shards(): pl.pallas_call(functools.partial(kernel, (peers, ax_peers, lines, cells,...]
where the time goes in v2:
time: 23.4 us; the launch traced here: 23.2 us
  Pallas kernels  19.3 us (82%)
  local copies, waits for them, and re-layouts  3.33 us (14%)
  between operations  0.65 us (3%)
    pallas_call x1, Pallas kernels, shards(): pl.pallas_call(functools.partial(kernel, (peers, ax_peers, lines, cells,...  19.3 us
    unnamed x7, local copies, waits for them, and re-layouts  3.33 us

profile of v2, /device:TPU:0, one launch (start us, length us, event | category | flops | bytes accessed | tf_op | source)
XLA Modules:
  0.0 23.2 jit_solution(441536548307058525)
XLA Ops:
  0.6 19.3 %shard_map.103 = (f32[24,8,256]{2,1,0:T(8,128)}, f32[24,8,256]{2,1,0:T(8,128)}, f32[24,8,256]{2,1,0:T(8,128)}) custom-call(f32[24,8,256]{2,1,0:T(8,128)} %bitcast.4, f32[96,256]{1,0:T(8,128)} %constant.14.clone.ends_hbm, f32[384,256]{1,0:T(8,128)} %constant.15.clone.local_hbm, f32[384,256]{1,0:T(8,128)} %constant.16.clone.halo_hbm, ...), custom_call_target="tpu_custom_call" | custom-call | tf_op jit(solution)/shard_map/pallas_call | solution.py:487
  19.9 0.0 copy-start.1
  19.9 1.7 %copy.14 = f32[3,8,8,256]{3,2,1,0:T(8,128)} copy(f32[3,8,8,256]{3,2,1,0:T(8,128)} %bitcast.7) | data formatting | bytes 393216
  21.6 0.0 copy-done.1
  21.6 0.0 copy-start
  21.6 0.7 %copy.15 = f32[3,8,8,256]{3,2,1,0:T(8,128)} copy(f32[3,8,8,256]{3,2,1,0:T(8,128)S(1)} %bitcast.6) | data formatting | bytes 393216
  22.2 0.3 %copy-done = f32[24,8,256]{2,1,0:T(8,128)S(1)} copy-done((f32[24,8,256]{2,1,0:T(8,128)S(1)}, f32[24,8,256]{2,1,0:T(8,128)}, u32[]{:S(2)}) %copy-start) | copy-done | bytes 196632
  22.6 0.7 %copy.16 = f32[3,8,8,256]{3,2,1,0:T(8,128)} copy(f32[3,8,8,256]{3,2,1,0:T(8,128)S(1)} %bitcast.5) | data formatting | bytes 393216
Async XLA Ops:
  19.9 1.7 %copy-start.1 = (f32[24,8,256]{2,1,0:T(8,128)S(1)}, f32[24,8,256]{2,1,0:T(8,128)}, u32[]{:S(2)}) copy-start(f32[24,8,256]{2,1,0:T(8,128)} %get-tuple-element.7) | copy-start | bytes 589828
  21.6 1.0 %copy-start = (f32[24,8,256]{2,1,0:T(8,128)S(1)}, f32[24,8,256]{2,1,0:T(8,128)}, u32[]{:S(2)}) copy-start(f32[24,8,256]{2,1,0:T(8,128)} %get-tuple-element.8) | copy-start | bytes 589828

commit v3 on v2

--- a/solution.py
+++ b/solution.py
@@ -451,6 +451,17 @@
         copy.wait_send()
 
 
+def finish(sources, targets, sems):
+    copies = [
+        pltpu.make_async_copy(source, target, sems.at[i])
+        for i, (source, target) in enumerate(zip(sources, targets))
+    ]
+    for copy in copies:
+        copy.start()
+    for copy in copies:
+        copy.wait()
+
+
 def shards(fields):
     peers, ax_peers = lax.axis_size("circ"), lax.axis_size("ax")
     components, radial, cells, width = fields.shape
@@ -461,7 +472,13 @@
     tables = [padded_table(table) for table in circ_tables(lines, cells, peers)]
     own, ax_ends, ax_apply = axial_tables(width, ax_peers)
     tables += [jnp.asarray(table, jnp.float32) for table in (own, ax_ends, ax_apply)]
-    out = jax.ShapeDtypeStruct((lines, cells, width), jnp.float32)
+    shape = (lines, cells, width)
+    out = jax.ShapeDtypeStruct(shape, jnp.float32)
+    inside = pltpu.VMEM(shape, jnp.float32)
+    operands = [
+        pltpu.with_memory_space_constraint(value, pltpu.HBM)
+        for value in (fields.reshape(shape), *tables)
+    ]
     scratch = [
         pltpu.VMEM((lines, cells, width), jnp.float32),
         *[pltpu.VMEM(table.shape, table.dtype) for table in tables[:4]],
@@ -484,16 +501,23 @@
         pltpu.SemaphoreType.DMA((ax_peers,)),
         pltpu.SemaphoreType.DMA((ax_peers,)),
     ]
-    results = pl.pallas_call(
+    held = pl.pallas_call(
         functools.partial(kernel, (peers, ax_peers, lines, cells, width, chunk)),
-        out_shape=(out, out, out),
+        out_shape=(inside,) * 3,
         in_specs=[pl.BlockSpec(memory_space=pltpu.HBM)] * 8,
         out_specs=[pl.BlockSpec(memory_space=pltpu.VMEM)] * 3,
         scratch_shapes=scratch,
         compiler_params=pltpu.CompilerParams(
-            collective_id=0, has_side_effects=True, vmem_limit_bytes=60 * 1024 * 1024
+            collective_id=0, has_side_effects=True, vmem_limit_bytes=24 * 1024 * 1024
         ),
-    )(fields.reshape(lines, cells, width), *tables)
+    )(*operands)
+    results = pl.pallas_call(
+        lambda a, b, c, x, y, z, sems: finish((a, b, c), (x, y, z), sems),
+        out_shape=(out,) * 3,
+        in_specs=[pl.BlockSpec(memory_space=pl.ANY)] * 3,
+        out_specs=[pl.BlockSpec(memory_space=pl.ANY)] * 3,
+        scratch_shapes=[pltpu.SemaphoreType.DMA((3,))],
+    )(*held)
     return tuple(result.reshape(fields.shape) for result in results)
 
 

time: 23.4 us -> 40.3 us (1.72)
  Pallas kernels: 19.3 us -> 37.4 us
  local copies, waits for them, and re-layouts: 3.33 us -> 2.04 us
    pallas_call x0 -> x1, Pallas kernels: none -> 19 us  [shards(): pl.pallas_call(lambda a, b, c, x, y, z, sems: finish((a, b, c), (x, y, z)...]
    unnamed x7 -> x6, local copies, waits for them, and re-layouts: 3.33 us -> 2.04 us
    pallas_call x1, Pallas kernels: 19.3 us -> 18.4 us  [shards(): pl.pallas_call(functools.partial(kernel, (peers, ax_peers, lines, cells,...]
where the time goes in v3:
time: 40.3 us; the launch traced here: 40.1 us
  Pallas kernels  37.4 us (93%)
  local copies, waits for them, and re-layouts  2.04 us (5%)
  between operations  0.65 us (2%)
    pallas_call x1, Pallas kernels, shards(): pl.pallas_call(lambda a, b, c, x, y, z, sems: finish((a, b, c), (x, y, z)...  19 us
    pallas_call x1, Pallas kernels, shards(): pl.pallas_call(functools.partial(kernel, (peers, ax_peers, lines, cells,...  18.4 us
    unnamed x6, local copies, waits for them, and re-layouts  2.04 us

profile of v3, /device:TPU:0, one launch (start us, length us, event | category | flops | bytes accessed | tf_op | source)
XLA Modules:
  0.0 40.1 jit_solution(16752379039803411721)
XLA Ops:
  0.6 18.4 %shard_map.103 = (f32[24,8,256]{2,1,0:T(8,128)S(1)}, f32[24,8,256]{2,1,0:T(8,128)S(1)}, f32[24,8,256]{2,1,0:T(8,128)S(1)}) custom-call(f32[24,8,256]{2,1,0:T(8,128)} %bitcast.4, f32[96,256]{1,0:T(8,128)} %constant.14.clone.ends_hbm, f32[384,256]{1,0:T(8,128)} %constant.15.clone.local_hbm, f32[384,256]{1,0:T(8,128)} %constant.16.clone.halo_hbm, ...), custom_call_target="tpu_custom_call" | custom-call | tf_op jit(solution)/shard_map/pallas_call | solution.py:504
  19.1 0.0 copy-start
  19.1 0.7 %copy-done = f32[24,8,256]{2,1,0:T(8,128)} copy-done((f32[24,8,256]{2,1,0:T(8,128)}, f32[24,8,256]{2,1,0:T(8,128)S(1)}, u32[]{:S(2)}) %copy-start) | copy-done | bytes 196632
  19.8 0.0 copy-start.1
  19.8 0.7 %copy-done.1 = f32[24,8,256]{2,1,0:T(8,128)} copy-done((f32[24,8,256]{2,1,0:T(8,128)}, f32[24,8,256]{2,1,0:T(8,128)S(1)}, u32[]{:S(2)}) %copy-start.1) | copy-done | bytes 196632
  20.4 0.0 copy-start.2
  20.4 0.7 %copy-done.2 = f32[24,8,256]{2,1,0:T(8,128)} copy-done((f32[24,8,256]{2,1,0:T(8,128)}, f32[24,8,256]{2,1,0:T(8,128)S(1)}, u32[]{:S(2)}) %copy-start.2) | copy-done | bytes 196632
  21.1 19.0 %shard_map.104 = (f32[24,8,256]{2,1,0:T(8,128)}, f32[24,8,256]{2,1,0:T(8,128)}, f32[24,8,256]{2,1,0:T(8,128)}) custom-call(f32[24,8,256]{2,1,0:T(8,128)} %copy-done, f32[24,8,256]{2,1,0:T(8,128)} %copy-done.1, f32[24,8,256]{2,1,0:T(8,128)} %copy-done.2), custom_call_target="tpu_custom_call" | custom-call | tf_op jit(solution)/shard_map/pallas_call | solution.py:514
Async XLA Ops:
  19.1 0.7 %copy-start = (f32[24,8,256]{2,1,0:T(8,128)}, f32[24,8,256]{2,1,0:T(8,128)S(1)}, u32[]{:S(2)}) copy-start(f32[24,8,256]{2,1,0:T(8,128)S(1)} %get-tuple-element.9.a) | copy-start | bytes 589828
  19.8 0.7 %copy-start.1 = (f32[24,8,256]{2,1,0:T(8,128)}, f32[24,8,256]{2,1,0:T(8,128)S(1)}, u32[]{:S(2)}) copy-start(f32[24,8,256]{2,1,0:T(8,128)S(1)} %get-tuple-element.10.b) | copy-start | bytes 589828
  20.4 0.7 %copy-start.2 = (f32[24,8,256]{2,1,0:T(8,128)}, f32[24,8,256]{2,1,0:T(8,128)S(1)}, u32[]{:S(2)}) copy-start(f32[24,8,256]{2,1,0:T(8,128)S(1)} %get-tuple-element.11.c) | copy-start | bytes 589828

commit v4 on v3

--- a/solution.py
+++ b/solution.py
@@ -517,7 +517,8 @@
         in_specs=[pl.BlockSpec(memory_space=pl.ANY)] * 3,
         out_specs=[pl.BlockSpec(memory_space=pl.ANY)] * 3,
         scratch_shapes=[pltpu.SemaphoreType.DMA((3,))],
-    )(*held)
+        compiler_params=pltpu.CompilerParams(vmem_limit_bytes=1024 * 1024),
+    )(*[pltpu.with_memory_space_constraint(value, pltpu.VMEM) for value in held])
     return tuple(result.reshape(fields.shape) for result in results)
 
 

time: 40.3 us -> 20.1 us (0.50)
  Pallas kernels: 37.4 us -> 19.3 us
  local copies, waits for them, and re-layouts: 2.04 us -> 0 us
    pallas_call x1, Pallas kernels: 19 us -> 0.83 us  [shards(): pl.pallas_call(lambda a, b, c, x, y, z, sems: finish((a, b, c), (x, y, z)...]
    unnamed x6 -> x0, local copies, waits for them, and re-layouts: 2.04 us -> none
where the time goes in v4:
time: 20.1 us; the launch traced here: 19.9 us
  Pallas kernels  19.3 us (96%)
  between operations  0.64 us (3%)
    pallas_call x1, Pallas kernels, shards(): pl.pallas_call(functools.partial(kernel, (peers, ax_peers, lines, cells,...  18.4 us
    pallas_call x1, Pallas kernels, shards(): pl.pallas_call(lambda a, b, c, x, y, z, sems: finish((a, b, c), (x, y, z)...  0.83 us

profile of v4, /device:TPU:0, one launch (start us, length us, event | category | flops | bytes accessed | tf_op | source)
XLA Modules:
  0.0 19.9 jit_solution(12687267413559042191)
XLA Ops:
  0.6 18.4 %shard_map.103 = (f32[24,8,256]{2,1,0:T(8,128)S(1)}, f32[24,8,256]{2,1,0:T(8,128)S(1)}, f32[24,8,256]{2,1,0:T(8,128)S(1)}) custom-call(f32[24,8,256]{2,1,0:T(8,128)} %bitcast.4, f32[96,256]{1,0:T(8,128)} %constant.14.clone.ends_hbm, f32[384,256]{1,0:T(8,128)} %constant.15.clone.local_hbm, f32[384,256]{1,0:T(8,128)} %constant.16.clone.halo_hbm, ...), custom_call_target="tpu_custom_call" | custom-call | tf_op jit(solution)/shard_map/pallas_call | solution.py:504
  19.1 0.8 %shard_map.104 = (f32[24,8,256]{2,1,0:T(8,128)}, f32[24,8,256]{2,1,0:T(8,128)}, f32[24,8,256]{2,1,0:T(8,128)}) custom-call(f32[24,8,256]{2,1,0:T(8,128)S(1)} %get-tuple-element.9.a, f32[24,8,256]{2,1,0:T(8,128)S(1)} %get-tuple-element.10.b, f32[24,8,256]{2,1,0:T(8,128)S(1)} %get-tuple-element.11.c), custom_call_target="tpu_custom_call" | custom-call | tf_op jit(solution)/shard_map/pallas_call | solution.py:514

commit v5 on v4

--- a/solution.py
+++ b/solution.py
@@ -299,8 +299,9 @@
 
     pl.semaphore_wait(barrier, peers - 1 + ax_peers - 1)
 
+    order = sorted(range(1, peers), key=lambda k: -min(k, peers - k))
     gathers = []
-    for k in range(1, peers):
+    for k in order:
         copy = pltpu.make_async_remote_copy(
             src_ref=outgoing.at[pl.ds(others[k] * chunk, chunk)],
             dst_ref=gathered.at[here],
@@ -320,18 +321,20 @@
     halo_out[1] = jnp.where(
         row < HALO, initial[:half_lines], pltpu.roll(initial[half_lines:], HALO, 1)
     )
+    odd = lax.rem(here, 2)
     halos = []
-    for side, target in ((0, others[1]), (1, others[peers - 1])):
-        copy = pltpu.make_async_remote_copy(
-            src_ref=halo_out.at[side],
-            dst_ref=halo_in.at[side],
-            send_sem=halo_send.at[side],
-            recv_sem=halo_recv.at[side],
-            device_id={"circ": target},
-            device_id_type=MESH,
-        )
-        copy.start()
-        halos.append(copy)
+    for side, step in ((1 - odd, 1 + (1 - odd) * (peers - 2)), (odd, 1 + odd * (peers - 2))):
+        halos.append(
+            pltpu.make_async_remote_copy(
+                src_ref=halo_out.at[side],
+                dst_ref=halo_in.at[side],
+                send_sem=halo_send.at[side],
+                recv_sem=halo_recv.at[side],
+                device_id={"circ": lax.rem(here + step, peers)},
+                device_id_type=MESH,
+            )
+        )
+    halos[0].start()
 
     loads[2].wait()
     ax_sums = precise_dot(ax_ends_table[...], flat, ((1,), (1,)))
@@ -376,7 +379,7 @@
         for kind in kinds
     ]
     returns = []
-    for k in range(peers):
+    for k in order + [0]:
         for tile in range(chunk):
             total = None
             for j in range(peers):
@@ -400,6 +403,7 @@
         )
         copy.start()
         returns.append(copy)
+    halos[1].start()
 
     loads[4].wait()
     axial = dot(data_parts(flat, 1), table_parts(own_table[...], 0))

time: 20.1 us -> 18.7 us (0.930)
  Pallas kernels: 19.3 us -> 17.9 us
    pallas_call x1, Pallas kernels: 18.4 us -> 17.1 us  [shards(): pl.pallas_call(functools.partial(kernel, (peers, ax_peers, lines, cells,...]
where the time goes in v5:
time: 18.7 us; the launch traced here: 18.6 us
  Pallas kernels  17.9 us (96%)
  between operations  0.64 us (3%)
    pallas_call x1, Pallas kernels, shards(): pl.pallas_call(functools.partial(kernel, (peers, ax_peers, lines, cells,...  17.1 us
    pallas_call x1, Pallas kernels, shards(): pl.pallas_call(lambda a, b, c, x, y, z, sems: finish((a, b, c), (x, y, z)...  0.83 us

profile of v5, /device:TPU:0, one launch (start us, length us, event | category | flops | bytes accessed | tf_op | source)
XLA Modules:
  0.0 18.6 jit_solution(14956136993302779259)
XLA Ops:
  0.6 17.1 %shard_map.103 = (f32[24,8,256]{2,1,0:T(8,128)S(1)}, f32[24,8,256]{2,1,0:T(8,128)S(1)}, f32[24,8,256]{2,1,0:T(8,128)S(1)}) custom-call(f32[24,8,256]{2,1,0:T(8,128)} %bitcast.4, f32[96,256]{1,0:T(8,128)} %constant.14.clone.ends_hbm, f32[384,256]{1,0:T(8,128)} %constant.15.clone.local_hbm, f32[384,256]{1,0:T(8,128)} %constant.16.clone.halo_hbm, ...), custom_call_target="tpu_custom_call" | custom-call | tf_op jit(solution)/shard_map/pallas_call | solution.py:508
  17.7 0.8 %shard_map.104 = (f32[24,8,256]{2,1,0:T(8,128)}, f32[24,8,256]{2,1,0:T(8,128)}, f32[24,8,256]{2,1,0:T(8,128)}) custom-call(f32[24,8,256]{2,1,0:T(8,128)S(1)} %get-tuple-element.9.a, f32[24,8,256]{2,1,0:T(8,128)S(1)} %get-tuple-element.10.b, f32[24,8,256]{2,1,0:T(8,128)S(1)} %get-tuple-element.11.c), custom_call_target="tpu_custom_call" | custom-call | tf_op jit(solution)/shard_map/pallas_call | solution.py:518

commit v6 on v5

--- a/solution.py
+++ b/solution.py
@@ -235,6 +235,8 @@
     outgoing,
     gathered,
     combined,
+    half_out,
+    half_in,
     incoming,
     halo_out,
     halo_in,
@@ -243,6 +245,7 @@
     load_sems,
     gather_send,
     gather_recv,
+    swap_sems,
     return_send,
     return_recv,
     halo_send,
@@ -256,6 +259,10 @@
     halves = width // 128
     row_blocks = 4 * lines // 8
     others = [lax.rem(here + k, peers) for k in range(peers)]
+    group = peers // 2
+    mine = lax.rem(here, group)
+    base = here - mine
+    mates = [lax.rem(mine + k, group) for k in range(group)]
     ax_others = [lax.rem(place + k, ax_peers) for k in range(ax_peers)]
 
     loads = [
@@ -292,22 +299,21 @@
         outgoing[half * row_blocks : (half + 1) * row_blocks] = end_sums[
             :, half * 128 : (half + 1) * 128
         ].reshape(row_blocks, 8, 128)
-    if halves * row_blocks < peers * chunk:
+    if halves * row_blocks < group * chunk:
         outgoing[halves * row_blocks :] = jnp.zeros(
-            (peers * chunk - halves * row_blocks, 8, 128), jnp.float32
+            (group * chunk - halves * row_blocks, 8, 128), jnp.float32
         )
 
     pl.semaphore_wait(barrier, peers - 1 + ax_peers - 1)
 
-    order = sorted(range(1, peers), key=lambda k: -min(k, peers - k))
     gathers = []
-    for k in order:
+    for k in range(1, group):
         copy = pltpu.make_async_remote_copy(
-            src_ref=outgoing.at[pl.ds(others[k] * chunk, chunk)],
-            dst_ref=gathered.at[here],
+            src_ref=outgoing.at[pl.ds(mates[k] * chunk, chunk)],
+            dst_ref=gathered.at[mine],
             send_sem=gather_send.at[k],
-            recv_sem=gather_recv.at[here],
-            device_id={"circ": others[k]},
+            recv_sem=gather_recv.at[mine],
+            device_id={"circ": base + mates[k]},
             device_id_type=MESH,
         )
         copy.start()
@@ -359,51 +365,71 @@
     deriv_ref[...] = own_part[:rows].reshape(lines, cells, width)
     filter_ref[...] = block + own_part[rows:].reshape(lines, cells, width)
 
-    for k in range(1, peers):
-        source = others[k]
+    for k in range(1, group):
         pltpu.make_async_remote_copy(
-            src_ref=gathered.at[source],
-            dst_ref=gathered.at[source],
+            src_ref=gathered.at[mates[k]],
+            dst_ref=gathered.at[mates[k]],
             send_sem=gather_send.at[k],
-            recv_sem=gather_recv.at[source],
-            device_id={"circ": source},
+            recv_sem=gather_recv.at[mates[k]],
+            device_id={"circ": base + mates[k]},
             device_id_type=MESH,
         ).wait_recv()
-    gathered[here] = outgoing[pl.ds(here * chunk, chunk)]
+    gathered[mine] = outgoing[pl.ds(mine * chunk, chunk)]
     kind_tiles = lines // 8
     kinds = [
-        lax.rem(here * chunk + tile, row_blocks) // kind_tiles for tile in range(chunk)
+        lax.rem(lax.rem(mine * chunk + tile, row_blocks) // kind_tiles, 4)
+        for tile in range(chunk)
     ]
-    factors = [
-        [carry_factor(kind, (k - 1) % peers, peers - 1 - k, cells) for k in range(peers)]
-        for kind in kinds
-    ]
-    returns = []
-    for k in order + [0]:
+    for tile in range(chunk):
+        half_sum = None
+        for source in range(group):
+            factor = carry_factor(kinds[tile], group - 1 - source, source, cells)
+            term = factor * gathered[source, tile]
+            half_sum = term if half_sum is None else half_sum + term
+        half_out[tile] = half_sum
+    swap = pltpu.make_async_remote_copy(
+        src_ref=half_out,
+        dst_ref=half_in,
+        send_sem=swap_sems.at[0],
+        recv_sem=swap_sems.at[1],
+        device_id={"circ": lax.rem(here + group, peers)},
+        device_id_type=MESH,
+    )
+    swap.start()
+    for target in range(group):
         for tile in range(chunk):
             total = None
-            for j in range(peers):
-                if j == k:
+            for source in range(group):
+                if source == target:
                     continue
-                term = factors[tile][(k - j) % peers] * gathered[others[j], tile]
+                factor = carry_factor(
+                    kinds[tile],
+                    (target - source - 1) % peers,
+                    (source - target - 1) % peers,
+                    cells,
+                )
+                term = factor * gathered[source, tile]
                 total = term if total is None else total + term
-            if k == 0:
-                incoming[here * chunk + tile] = total
-            else:
-                combined[k, tile] = total
-        if k == 0:
-            continue
+            combined[target, tile] = total
+    swap.wait_recv()
+    for target in range(group):
+        for tile in range(chunk):
+            factor = carry_factor(kinds[tile], target, group - 1 - target, cells)
+            combined[target, tile] += factor * half_in[tile]
+    returns = []
+    for k in range(1, group):
         copy = pltpu.make_async_remote_copy(
-            src_ref=combined.at[k],
-            dst_ref=incoming.at[pl.ds(here * chunk, chunk)],
+            src_ref=combined.at[mates[k]],
+            dst_ref=incoming.at[pl.ds(mine * chunk, chunk)],
             send_sem=return_send.at[k],
-            recv_sem=return_recv.at[here],
-            device_id={"circ": others[k]},
+            recv_sem=return_recv.at[mine],
+            device_id={"circ": base + mates[k]},
             device_id_type=MESH,
         )
         copy.start()
         returns.append(copy)
     halos[1].start()
+    incoming[pl.ds(mine * chunk, chunk)] = combined[mine]
 
     loads[4].wait()
     axial = dot(data_parts(flat, 1), table_parts(own_table[...], 0))
@@ -430,14 +456,13 @@
     filter_ref[...] += edge[rows:].reshape(lines, cells, width)
 
     loads[7].wait()
-    for k in range(1, peers):
-        source = others[k]
+    for k in range(1, group):
         pltpu.make_async_remote_copy(
-            src_ref=combined.at[k],
-            dst_ref=incoming.at[pl.ds(source * chunk, chunk)],
+            src_ref=combined.at[mates[k]],
+            dst_ref=incoming.at[pl.ds(mates[k] * chunk, chunk)],
             send_sem=return_send.at[k],
-            recv_sem=return_recv.at[source],
-            device_id={"circ": source},
+            recv_sem=return_recv.at[mates[k]],
+            device_id={"circ": base + mates[k]},
             device_id_type=MESH,
         ).wait_recv()
     entering = jnp.concatenate(
@@ -451,7 +476,7 @@
     deriv_ref[...] += carried[:rows].reshape(lines, cells, width)
     filter_ref[...] += carried[rows:].reshape(lines, cells, width)
 
-    for copy in gathers + ax_copies + halos + returns:
+    for copy in gathers + ax_copies + halos + returns + [swap]:
         copy.wait_send()
 
 
@@ -472,7 +497,8 @@
     lines = components * radial
     halves = width // 128
     tiles = halves * 4 * lines // 8
-    chunk = -(-tiles // peers)
+    group = peers // 2
+    chunk = -(-tiles // group)
     tables = [padded_table(table) for table in circ_tables(lines, cells, peers)]
     own, ax_ends, ax_apply = axial_tables(width, ax_peers)
     tables += [jnp.asarray(table, jnp.float32) for table in (own, ax_ends, ax_apply)]
@@ -487,19 +513,22 @@
         pltpu.VMEM((lines, cells, width), jnp.float32),
         *[pltpu.VMEM(table.shape, table.dtype) for table in tables[:4]],
         *[pltpu.VMEM(table.shape[1:], table.dtype) for table in tables[4:]],
-        pltpu.VMEM((peers * chunk, 8, 128), jnp.float32),
-        pltpu.VMEM((peers, chunk, 8, 128), jnp.float32),
-        pltpu.VMEM((peers, chunk, 8, 128), jnp.float32),
-        pltpu.VMEM((peers * chunk, 8, 128), jnp.float32),
+        pltpu.VMEM((group * chunk, 8, 128), jnp.float32),
+        pltpu.VMEM((group, chunk, 8, 128), jnp.float32),
+        pltpu.VMEM((group, chunk, 8, 128), jnp.float32),
+        pltpu.VMEM((chunk, 8, 128), jnp.float32),
+        pltpu.VMEM((chunk, 8, 128), jnp.float32),
+        pltpu.VMEM((group * chunk, 8, 128), jnp.float32),
         pltpu.VMEM((2, lines // 2, 8, width), jnp.float32),
         pltpu.VMEM((2, lines // 2, 8, width), jnp.float32),
         pltpu.VMEM((8, lines * cells), jnp.float32),
         pltpu.VMEM((ax_peers, 8, lines * cells), jnp.float32),
         pltpu.SemaphoreType.DMA((8,)),
-        pltpu.SemaphoreType.DMA((peers,)),
-        pltpu.SemaphoreType.DMA((peers,)),
-        pltpu.SemaphoreType.DMA((peers,)),
-        pltpu.SemaphoreType.DMA((peers,)),
+        pltpu.SemaphoreType.DMA((group,)),
+        pltpu.SemaphoreType.DMA((group,)),
+        pltpu.SemaphoreType.DMA((2,)),
+        pltpu.SemaphoreType.DMA((group,)),
+        pltpu.SemaphoreType.DMA((group,)),
         pltpu.SemaphoreType.DMA((2,)),
         pltpu.SemaphoreType.DMA((2,)),
         pltpu.SemaphoreType.DMA((ax_peers,)),

time: 18.7 us -> 19.2 us (1.027)
  Pallas kernels: 17.9 us -> 18.4 us
    pallas_call x1, Pallas kernels: 17.1 us -> 17.5 us  [shards(): pl.pallas_call(functools.partial(kernel, (peers, ax_peers, lines, cells,...]
where the time goes in v6:
time: 19.2 us; the launch traced here: 19 us
  Pallas kernels  18.4 us (96%)
  between operations  0.64 us (3%)
    pallas_call x1, Pallas kernels, shards(): pl.pallas_call(functools.partial(kernel, (peers, ax_peers, lines, cells,...  17.5 us
    pallas_call x1, Pallas kernels, shards(): pl.pallas_call(lambda a, b, c, x, y, z, sems: finish((a, b, c), (x, y, z)...  0.83 us

profile of v6, /device:TPU:0, one launch (start us, length us, event | category | flops | bytes accessed | tf_op | source)
XLA Modules:
  0.0 19.0 jit_solution(15934899683751201349)
XLA Ops:
  0.6 17.5 %shard_map.103 = (f32[24,8,256]{2,1,0:T(8,128)S(1)}, f32[24,8,256]{2,1,0:T(8,128)S(1)}, f32[24,8,256]{2,1,0:T(8,128)S(1)}) custom-call(f32[24,8,256]{2,1,0:T(8,128)} %bitcast.4, f32[96,256]{1,0:T(8,128)} %constant.14.clone.ends_hbm, f32[384,256]{1,0:T(8,128)} %constant.15.clone.local_hbm, f32[384,256]{1,0:T(8,128)} %constant.16.clone.halo_hbm, ...), custom_call_target="tpu_custom_call" | custom-call | tf_op jit(solution)/shard_map/pallas_call | solution.py:537
  18.2 0.8 %shard_map.104 = (f32[24,8,256]{2,1,0:T(8,128)}, f32[24,8,256]{2,1,0:T(8,128)}, f32[24,8,256]{2,1,0:T(8,128)}) custom-call(f32[24,8,256]{2,1,0:T(8,128)S(1)} %get-tuple-element.9.a, f32[24,8,256]{2,1,0:T(8,128)S(1)} %get-tuple-element.10.b, f32[24,8,256]{2,1,0:T(8,128)S(1)} %get-tuple-element.11.c), custom_call_target="tpu_custom_call" | custom-call | tf_op jit(solution)/shard_map/pallas_call | solution.py:547

commit v7 on v5

--- a/solution.py
+++ b/solution.py
@@ -81,7 +81,7 @@
                 base = 2 * HALO * (line % (lines // 2)) + HALO * (line // (lines // 2))
                 table[line * cells : (line + 1) * cells, base : base + HALO] = side
             spread.append(table)
-        halo.append(np.concatenate(spread, axis=1))
+        halo.append(spread)
         ends.append(np.kron(eye, (root ** (cells - 1 - steps))[None, :]))
         ends.append(np.kron(eye, (root**steps)[None, :]))
         up = np.kron(eye, (sign * gain * root ** (steps + 1.0))[:, None])
@@ -98,7 +98,7 @@
     return (
         np.concatenate(ends, axis=0),
         np.concatenate(local, axis=0),
-        np.concatenate(halo, axis=0),
+        [np.concatenate([halo[0][i], halo[1][i]], axis=0) for i in range(2)],
         from_ends,
     )
 
@@ -273,14 +273,14 @@
             )
         )
     ]
-    for load in loads:
-        load.start()
-
     barrier = pltpu.get_barrier_semaphore()
     for k in range(1, peers):
         pl.semaphore_signal(barrier, inc=1, device_id={"circ": others[k]}, device_id_type=MESH)
     for k in range(1, ax_peers):
         pl.semaphore_signal(barrier, inc=1, device_id={"ax": ax_others[k]}, device_id_type=MESH)
+
+    for load in loads:
+        load.start()
 
     loads[0].wait()
     loads[1].wait()
@@ -422,12 +422,23 @@
     axial = axial + precise_dot(received, ax_apply_table[...], ((0,), (0,)))
     axial_ref[...] = axial.reshape(lines, cells, width)
 
+    def add_edge(side):
+        table = table_parts(halo_table[side], 1)
+        edge = dot(table, data_parts(halo_in[side].reshape(lines * HALO, width), 0))
+        deriv_ref[...] += edge[:rows].reshape(lines, cells, width)
+        filter_ref[...] += edge[rows:].reshape(lines, cells, width)
+
     loads[5].wait()
-    for copy in halos:
-        copy.wait_recv()
-    edge = dot(table_parts(halo_table[...], 1), data_parts(halo_in[...].reshape(2 * lines * HALO, width), 0))
-    deriv_ref[...] += edge[:rows].reshape(lines, cells, width)
-    filter_ref[...] += edge[rows:].reshape(lines, cells, width)
+    halos[0].wait_send()
+    pltpu.make_async_remote_copy(
+        src_ref=halo_out.at[odd],
+        dst_ref=halo_in.at[odd],
+        send_sem=halo_send.at[odd],
+        recv_sem=halo_recv.at[odd],
+        device_id={"circ": lax.rem(here + 1 + odd * (peers - 2), peers)},
+        device_id_type=MESH,
+    ).wait_recv()
+    add_edge(odd)
 
     loads[7].wait()
     for k in range(1, peers):
@@ -451,7 +462,18 @@
     deriv_ref[...] += carried[:rows].reshape(lines, cells, width)
     filter_ref[...] += carried[rows:].reshape(lines, cells, width)
 
-    for copy in gathers + ax_copies + halos + returns:
+    halos[1].wait_send()
+    pltpu.make_async_remote_copy(
+        src_ref=halo_out.at[1 - odd],
+        dst_ref=halo_in.at[1 - odd],
+        send_sem=halo_send.at[1 - odd],
+        recv_sem=halo_recv.at[1 - odd],
+        device_id={"circ": lax.rem(here + 1 + (1 - odd) * (peers - 2), peers)},
+        device_id_type=MESH,
+    ).wait_recv()
+    add_edge(1 - odd)
+
+    for copy in gathers + ax_copies + returns:
         copy.wait_send()
 
 
@@ -473,7 +495,9 @@
     halves = width // 128
     tiles = halves * 4 * lines // 8
     chunk = -(-tiles // peers)
-    tables = [padded_table(table) for table in circ_tables(lines, cells, peers)]
+    ends, local, halo, from_ends = circ_tables(lines, cells, peers)
+    halo = jnp.stack([padded_table(side) for side in halo])
+    tables = [padded_table(ends), padded_table(local), halo, padded_table(from_ends)]
     own, ax_ends, ax_apply = axial_tables(width, ax_peers)
     tables += [jnp.asarray(table, jnp.float32) for table in (own, ax_ends, ax_apply)]
     shape = (lines, cells, width)

time: 18.7 us -> 18.9 us (1.011)
  Pallas kernels: 17.9 us -> 18.1 us
    pallas_call x1, Pallas kernels: 17.1 us -> 17.3 us  [shards(): pl.pallas_call(functools.partial(kernel, (peers, ax_peers, lines, cells,...]
where the time goes in v7:
time: 18.9 us; the launch traced here: 18.8 us
  Pallas kernels  18.1 us (96%)
  between operations  0.64 us (3%)
    pallas_call x1, Pallas kernels, shards(): pl.pallas_call(functools.partial(kernel, (peers, ax_peers, lines, cells,...  17.3 us
    pallas_call x1, Pallas kernels, shards(): pl.pallas_call(lambda a, b, c, x, y, z, sems: finish((a, b, c), (x, y, z)...  0.83 us

profile of v7, /device:TPU:0, one launch (start us, length us, event | category | flops | bytes accessed | tf_op | source)
XLA Modules:
  0.0 18.8 jit_solution(8049403515824572528)
XLA Ops:
  0.6 17.3 %shard_map.112 = (f32[24,8,256]{2,1,0:T(8,128)S(1)}, f32[24,8,256]{2,1,0:T(8,128)S(1)}, f32[24,8,256]{2,1,0:T(8,128)S(1)}) custom-call(f32[24,8,256]{2,1,0:T(8,128)} %bitcast.4, f32[96,256]{1,0:T(8,128)} %constant.18.clone.ends_hbm, f32[384,256]{1,0:T(8,128)} %constant.19.clone.local_hbm, f32[2,384,128]{2,1,0:T(8,128)} %constant.26.halo_hbm, ...), custom_call_target="tpu_custom_call" | custom-call | tf_op jit(solution)/shard_map/pallas_call | solution.py:532
  17.9 0.8 %shard_map.113 = (f32[24,8,256]{2,1,0:T(8,128)}, f32[24,8,256]{2,1,0:T(8,128)}, f32[24,8,256]{2,1,0:T(8,128)}) custom-call(f32[24,8,256]{2,1,0:T(8,128)S(1)} %get-tuple-element.9.a, f32[24,8,256]{2,1,0:T(8,128)S(1)} %get-tuple-element.10.b, f32[24,8,256]{2,1,0:T(8,128)S(1)} %get-tuple-element.11.c), custom_call_target="tpu_custom_call" | custom-call | tf_op jit(solution)/shard_map/pallas_call | solution.py:542

commit v8 on v7

--- a/solution.py
+++ b/solution.py
@@ -353,12 +353,7 @@
         copy.start()
         ax_copies.append(copy)
 
-    loads[3].wait()
     rows = lines * cells
-    own_part = dot(table_parts(local_table[...], 1), tall)
-    deriv_ref[...] = own_part[:rows].reshape(lines, cells, width)
-    filter_ref[...] = block + own_part[rows:].reshape(lines, cells, width)
-
     for k in range(1, peers):
         source = others[k]
         pltpu.make_async_remote_copy(
@@ -404,6 +399,11 @@
         copy.start()
         returns.append(copy)
     halos[1].start()
+
+    loads[3].wait()
+    own_part = dot(table_parts(local_table[...], 1), tall)
+    deriv_ref[...] = own_part[:rows].reshape(lines, cells, width)
+    filter_ref[...] = block + own_part[rows:].reshape(lines, cells, width)
 
     loads[4].wait()
     axial = dot(data_parts(flat, 1), table_parts(own_table[...], 0))

time: 18.9 us -> 18.9 us (level)
  no operation moved by 1% of the time
where the time goes in v8:
time: 18.9 us; the launch traced here: 18.8 us
  Pallas kernels  18.1 us (96%)
  between operations  0.64 us (3%)
    pallas_call x1, Pallas kernels, shards(): pl.pallas_call(functools.partial(kernel, (peers, ax_peers, lines, cells,...  17.3 us
    pallas_call x1, Pallas kernels, shards(): pl.pallas_call(lambda a, b, c, x, y, z, sems: finish((a, b, c), (x, y, z)...  0.83 us

profile of v8, /device:TPU:0, one launch (start us, length us, event | category | flops | bytes accessed | tf_op | source)
XLA Modules:
  0.0 18.8 jit_solution(13844628433239360785)
XLA Ops:
  0.6 17.3 %shard_map.112 = (f32[24,8,256]{2,1,0:T(8,128)S(1)}, f32[24,8,256]{2,1,0:T(8,128)S(1)}, f32[24,8,256]{2,1,0:T(8,128)S(1)}) custom-call(f32[24,8,256]{2,1,0:T(8,128)} %bitcast.4, f32[96,256]{1,0:T(8,128)} %constant.18.clone.ends_hbm, f32[384,256]{1,0:T(8,128)} %constant.19.clone.local_hbm, f32[2,384,128]{2,1,0:T(8,128)} %constant.26.halo_hbm, ...), custom_call_target="tpu_custom_call" | custom-call | tf_op jit(solution)/shard_map/pallas_call | solution.py:532
  17.9 0.8 %shard_map.113 = (f32[24,8,256]{2,1,0:T(8,128)}, f32[24,8,256]{2,1,0:T(8,128)}, f32[24,8,256]{2,1,0:T(8,128)}) custom-call(f32[24,8,256]{2,1,0:T(8,128)S(1)} %get-tuple-element.9.a, f32[24,8,256]{2,1,0:T(8,128)S(1)} %get-tuple-element.10.b, f32[24,8,256]{2,1,0:T(8,128)S(1)} %get-tuple-element.11.c), custom_call_target="tpu_custom_call" | custom-call | tf_op jit(solution)/shard_map/pallas_call | solution.py:542

commit v9 on v8

--- a/solution.py
+++ b/solution.py
@@ -334,7 +334,6 @@
                 device_id_type=MESH,
             )
         )
-    halos[0].start()
 
     loads[2].wait()
     ax_sums = precise_dot(ax_ends_table[...], flat, ((1,), (1,)))
@@ -398,6 +397,7 @@
         )
         copy.start()
         returns.append(copy)
+    halos[0].start()
     halos[1].start()
 
     loads[3].wait()

time: 18.9 us -> 19.6 us (1.037)
  Pallas kernels: 18.1 us -> 18.8 us
    pallas_call x1, Pallas kernels: 17.3 us -> 17.9 us  [shards(): pl.pallas_call(functools.partial(kernel, (peers, ax_peers, lines, cells,...]
where the time goes in v9:
time: 19.6 us; the launch traced here: 19.4 us
  Pallas kernels  18.8 us (96%)
  between operations  0.64 us (3%)
    pallas_call x1, Pallas kernels, shards(): pl.pallas_call(functools.partial(kernel, (peers, ax_peers, lines, cells,...  17.9 us
    pallas_call x1, Pallas kernels, shards(): pl.pallas_call(lambda a, b, c, x, y, z, sems: finish((a, b, c), (x, y, z)...  0.83 us

profile of v9, /device:TPU:0, one launch (start us, length us, event | category | flops | bytes accessed | tf_op | source)
XLA Modules:
  0.0 19.4 jit_solution(11336554574209352549)
XLA Ops:
  0.6 17.9 %shard_map.112 = (f32[24,8,256]{2,1,0:T(8,128)S(1)}, f32[24,8,256]{2,1,0:T(8,128)S(1)}, f32[24,8,256]{2,1,0:T(8,128)S(1)}) custom-call(f32[24,8,256]{2,1,0:T(8,128)} %bitcast.4, f32[96,256]{1,0:T(8,128)} %constant.18.clone.ends_hbm, f32[384,256]{1,0:T(8,128)} %constant.19.clone.local_hbm, f32[2,384,128]{2,1,0:T(8,128)} %constant.26.halo_hbm, ...), custom_call_target="tpu_custom_call" | custom-call | tf_op jit(solution)/shard_map/pallas_call | solution.py:532
  18.6 0.8 %shard_map.113 = (f32[24,8,256]{2,1,0:T(8,128)}, f32[24,8,256]{2,1,0:T(8,128)}, f32[24,8,256]{2,1,0:T(8,128)}) custom-call(f32[24,8,256]{2,1,0:T(8,128)S(1)} %get-tuple-element.9.a, f32[24,8,256]{2,1,0:T(8,128)S(1)} %get-tuple-element.10.b, f32[24,8,256]{2,1,0:T(8,128)S(1)} %get-tuple-element.11.c), custom_call_target="tpu_custom_call" | custom-call | tf_op jit(solution)/shard_map/pallas_call | solution.py:542

commit v10 on v9

--- a/solution.py
+++ b/solution.py
@@ -335,6 +335,8 @@
             )
         )
 
+    pl.when(lax.rem(place, 2) == 0)(halos[0].start)
+
     loads[2].wait()
     ax_sums = precise_dot(ax_ends_table[...], flat, ((1,), (1,)))
     ax_out[...] = ax_sums
@@ -397,7 +399,7 @@
         )
         copy.start()
         returns.append(copy)
-    halos[0].start()
+    pl.when(lax.rem(place, 2) == 1)(halos[0].start)
     halos[1].start()
 
     loads[3].wait()

time: 19.6 us -> 18.3 us (0.934)
  Pallas kernels: 18.8 us -> 17.5 us
    pallas_call x1, Pallas kernels: 17.9 us -> 16.6 us  [shards(): pl.pallas_call(functools.partial(kernel, (peers, ax_peers, lines, cells,...]
where the time goes in v10:
time: 18.3 us; the launch traced here: 18.1 us
  Pallas kernels  17.5 us (96%)
  between operations  0.64 us (3%)
    pallas_call x1, Pallas kernels, shards(): pl.pallas_call(functools.partial(kernel, (peers, ax_peers, lines, cells,...  16.6 us
    pallas_call x1, Pallas kernels, shards(): pl.pallas_call(lambda a, b, c, x, y, z, sems: finish((a, b, c), (x, y, z)...  0.83 us

profile of v10, /device:TPU:0, one launch (start us, length us, event | category | flops | bytes accessed | tf_op | source)
XLA Modules:
  0.0 18.1 jit_solution(7282027400809666384)
XLA Ops:
  0.6 16.6 %shard_map.112 = (f32[24,8,256]{2,1,0:T(8,128)S(1)}, f32[24,8,256]{2,1,0:T(8,128)S(1)}, f32[24,8,256]{2,1,0:T(8,128)S(1)}) custom-call(f32[24,8,256]{2,1,0:T(8,128)} %bitcast.4, f32[96,256]{1,0:T(8,128)} %constant.18.clone.ends_hbm, f32[384,256]{1,0:T(8,128)} %constant.19.clone.local_hbm, f32[2,384,128]{2,1,0:T(8,128)} %constant.26.halo_hbm, ...), custom_call_target="tpu_custom_call" | custom-call | tf_op jit(solution)/shard_map/pallas_call | solution.py:534
  17.3 0.8 %shard_map.113 = (f32[24,8,256]{2,1,0:T(8,128)}, f32[24,8,256]{2,1,0:T(8,128)}, f32[24,8,256]{2,1,0:T(8,128)}) custom-call(f32[24,8,256]{2,1,0:T(8,128)S(1)} %get-tuple-element.9.a, f32[24,8,256]{2,1,0:T(8,128)S(1)} %get-tuple-element.10.b, f32[24,8,256]{2,1,0:T(8,128)S(1)} %get-tuple-element.11.c), custom_call_target="tpu_custom_call" | custom-call | tf_op jit(solution)/shard_map/pallas_call | solution.py:544

commit v11 on v9

--- a/solution.py
+++ b/solution.py
@@ -335,6 +335,12 @@
             )
         )
 
+    def start_halos():
+        halos[0].start()
+        halos[1].start()
+
+    pl.when(lax.rem(place, 2) == 0)(start_halos)
+
     loads[2].wait()
     ax_sums = precise_dot(ax_ends_table[...], flat, ((1,), (1,)))
     ax_out[...] = ax_sums
@@ -397,8 +403,7 @@
         )
         copy.start()
         returns.append(copy)
-    halos[0].start()
-    halos[1].start()
+    pl.when(lax.rem(place, 2) == 1)(start_halos)
 
     loads[3].wait()
     own_part = dot(table_parts(local_table[...], 1), tall)

time: 19.6 us -> 18.3 us (0.934)
  Pallas kernels: 18.8 us -> 17.5 us
    pallas_call x1, Pallas kernels: 17.9 us -> 16.6 us  [shards(): pl.pallas_call(functools.partial(kernel, (peers, ax_peers, lines, cells,...]
where the time goes in v11:
time: 18.3 us; the launch traced here: 18.1 us
  Pallas kernels  17.5 us (96%)
  between operations  0.64 us (3%)
    pallas_call x1, Pallas kernels, shards(): pl.pallas_call(functools.partial(kernel, (peers, ax_peers, lines, cells,...  16.6 us
    pallas_call x1, Pallas kernels, shards(): pl.pallas_call(lambda a, b, c, x, y, z, sems: finish((a, b, c), (x, y, z)...  0.83 us

profile of v11, /device:TPU:0, one launch (start us, length us, event | category | flops | bytes accessed | tf_op | source)
XLA Modules:
  0.0 18.1 jit_solution(8010251111928255187)
XLA Ops:
  0.6 16.6 %shard_map.112 = (f32[24,8,256]{2,1,0:T(8,128)S(1)}, f32[24,8,256]{2,1,0:T(8,128)S(1)}, f32[24,8,256]{2,1,0:T(8,128)S(1)}) custom-call(f32[24,8,256]{2,1,0:T(8,128)} %bitcast.4, f32[96,256]{1,0:T(8,128)} %constant.18.clone.ends_hbm, f32[384,256]{1,0:T(8,128)} %constant.19.clone.local_hbm, f32[2,384,128]{2,1,0:T(8,128)} %constant.26.halo_hbm, ...), custom_call_target="tpu_custom_call" | custom-call | tf_op jit(solution)/shard_map/pallas_call | solution.py:537
  17.3 0.8 %shard_map.113 = (f32[24,8,256]{2,1,0:T(8,128)}, f32[24,8,256]{2,1,0:T(8,128)}, f32[24,8,256]{2,1,0:T(8,128)}) custom-call(f32[24,8,256]{2,1,0:T(8,128)S(1)} %get-tuple-element.9.a, f32[24,8,256]{2,1,0:T(8,128)S(1)} %get-tuple-element.10.b, f32[24,8,256]{2,1,0:T(8,128)S(1)} %get-tuple-element.11.c), custom_call_target="tpu_custom_call" | custom-call | tf_op jit(solution)/shard_map/pallas_call | solution.py:547

commit v12 on v11

--- a/solution.py
+++ b/solution.py
@@ -445,6 +445,20 @@
     ).wait_recv()
     add_edge(odd)
 
+    def near_side():
+        halos[1].wait_send()
+        pltpu.make_async_remote_copy(
+            src_ref=halo_out.at[1 - odd],
+            dst_ref=halo_in.at[1 - odd],
+            send_sem=halo_send.at[1 - odd],
+            recv_sem=halo_recv.at[1 - odd],
+            device_id={"circ": lax.rem(here + 1 + (1 - odd) * (peers - 2), peers)},
+            device_id_type=MESH,
+        ).wait_recv()
+        add_edge(1 - odd)
+
+    pl.when(lax.rem(place, 2) == 0)(near_side)
+
     loads[7].wait()
     for k in range(1, peers):
         source = others[k]
@@ -467,16 +481,7 @@
     deriv_ref[...] += carried[:rows].reshape(lines, cells, width)
     filter_ref[...] += carried[rows:].reshape(lines, cells, width)
 
-    halos[1].wait_send()
-    pltpu.make_async_remote_copy(
-        src_ref=halo_out.at[1 - odd],
-        dst_ref=halo_in.at[1 - odd],
-        send_sem=halo_send.at[1 - odd],
-        recv_sem=halo_recv.at[1 - odd],
-        device_id={"circ": lax.rem(here + 1 + (1 - odd) * (peers - 2), peers)},
-        device_id_type=MESH,
-    ).wait_recv()
-    add_edge(1 - odd)
+    pl.when(lax.rem(place, 2) == 1)(near_side)
 
     for copy in gathers + ax_copies + returns:
         copy.wait_send()

time: 18.3 us -> 17.9 us (0.978)
  Pallas kernels: 17.5 us -> 17.1 us
    pallas_call x1, Pallas kernels: 16.6 us -> 16.3 us  [shards(): pl.pallas_call(functools.partial(kernel, (peers, ax_peers, lines, cells,...]
where the time goes in v12:
time: 17.9 us; the launch traced here: 17.8 us
  Pallas kernels  17.1 us (96%)
  between operations  0.64 us (4%)
    pallas_call x1, Pallas kernels, shards(): pl.pallas_call(functools.partial(kernel, (peers, ax_peers, lines, cells,...  16.3 us
    pallas_call x1, Pallas kernels, shards(): pl.pallas_call(lambda a, b, c, x, y, z, sems: finish((a, b, c), (x, y, z)...  0.83 us

profile of v12, /device:TPU:0, one launch (start us, length us, event | category | flops | bytes accessed | tf_op | source)
XLA Modules:
  0.0 17.8 jit_solution(6123129554779255299)
XLA Ops:
  0.6 16.3 %shard_map.112 = (f32[24,8,256]{2,1,0:T(8,128)S(1)}, f32[24,8,256]{2,1,0:T(8,128)S(1)}, f32[24,8,256]{2,1,0:T(8,128)S(1)}) custom-call(f32[24,8,256]{2,1,0:T(8,128)} %bitcast.4, f32[96,256]{1,0:T(8,128)} %constant.18.clone.ends_hbm, f32[384,256]{1,0:T(8,128)} %constant.19.clone.local_hbm, f32[2,384,128]{2,1,0:T(8,128)} %constant.26.halo_hbm, ...), custom_call_target="tpu_custom_call" | custom-call | tf_op jit(solution)/shard_map/pallas_call | solution.py:542
  16.9 0.8 %shard_map.113 = (f32[24,8,256]{2,1,0:T(8,128)}, f32[24,8,256]{2,1,0:T(8,128)}, f32[24,8,256]{2,1,0:T(8,128)}) custom-call(f32[24,8,256]{2,1,0:T(8,128)S(1)} %get-tuple-element.9.a, f32[24,8,256]{2,1,0:T(8,128)S(1)} %get-tuple-element.10.b, f32[24,8,256]{2,1,0:T(8,128)S(1)} %get-tuple-element.11.c), custom_call_target="tpu_custom_call" | custom-call | tf_op jit(solution)/shard_map/pallas_call | solution.py:552
